TPU v7x, 512 devices: a whole 4x4x16 slice. The times are simulated.
512 devices in a mesh: row: 32 (over z, x_hi), col: 16 (over x_lo, y, core).
Axes of the slice: x: 4 (x_hi: 2, x_lo: 2; x = x_hi * 2 + x_lo), y: 4, z: 16, core: 2. Of those that a mesh axis runs over, the one named last changes fastest.
Arguments:
- upper: float32 [1, 32, 6, 16, 128, 128], P(None, 'row', None, 'col'), may hold values from -1 to 1
- mask: int32 [1, 32, 6, 16], P(None, 'row', None, 'col'), may hold values from 0 to 1, as said below
Outputs:
- square: float32 [1, 32, 24, 16, 128, 128], P(None, 'row', None, 'col')
Inputs may be any that keep to these rules, and one draw needn't show every extreme that they name: A stored block is present where mask is 1; blocks on the main diagonal are always present.
All inputs are finite; a program needn't handle non-finite values.
Results may differ from a plain program's by a relative error of at most 0.0003.
Values sent between devices are 32-bit elements; how exact they have to be, the bound alone decides.
No kernel may reach another device: no remote copies, remote signals or barrier semaphores. Data moves between devices by JAX's collectives and lax.ppermute only.
A program may use at most 64 MiB of HBM per device.

v0:
```python
import jax
import jax.numpy as jnp
from jax import lax
from jax.sharding import PartitionSpec as P


def partner_2(block, axis, distance):
    count = lax.axis_size(axis)
    route = []
    for low in range(count):
        high = low | 1 << distance
        if high != low and high < count:
            route += [(low, high), (high, low)]
    return lax.ppermute(block, axis, route)


def shifted(block, axis, distance):
    devices = range(lax.axis_size(axis))
    route = [((i - distance) % len(devices), i) for i in devices]
    return lax.ppermute(block, axis, route)


def route(tile, sources, outward, inward):
    count = sources.shape[0]
    flat = tile.reshape(count, -1)
    held = outward(flat)
    held = jnp.take(held, sources, axis=0)
    return inward(held).reshape(tile.shape)


def lower_blocks(flipped, partner, row_at, col_at, row_count, col_count):
    local_rows = flipped.shape[0]
    slot_count = flipped.shape[1]
    slot_ids = jnp.arange(slot_count, dtype=jnp.int32)
    distance = slot_count - slot_ids
    source_row = row_at + col_at - col_count * distance
    layer_pick = distance % 2
    row_offset = jnp.floor_divide(source_row, row_count)
    source_slot = slot_count - slot_ids - jnp.where(col_at >= 1, 1, 0)
    present = (source_slot < slot_count).astype(jnp.float32)
    source_slot = jnp.minimum(source_slot, slot_count - 1)
    both_layers = jnp.stack([flipped, partner])
    local_ids = jnp.arange(local_rows, dtype=jnp.int32)

    def pick_block(layer_index, offset, column):
        chosen = lax.dynamic_index_in_dim(both_layers, layer_index, 0, keepdims=False)
        column_blocks = lax.dynamic_index_in_dim(chosen, column, 1, keepdims=False)
        return jnp.take(column_blocks, (local_ids + offset) % local_rows, axis=0)

    picked = jax.vmap(pick_block)(layer_pick, row_offset, source_slot)
    picked = jnp.swapaxes(picked, -1, -2) * present[:, None, None, None]
    return jnp.moveaxis(picked, 0, 1)


def accumulate(
    accumulated, left_blocks, right_tiles, step_number, row_at, col_at, row_count, col_count
):
    local_rows = left_blocks.shape[0]
    slot_pairs = left_blocks.shape[1]
    slot_count = slot_pairs // 2
    residue = row_at % col_count
    start_class = (col_at + step_number) % col_count
    right_class = (-residue - step_number) % col_count
    target_class = (col_at - residue) % col_count
    carry_over = (start_class + right_class - target_class) // col_count
    base_row = (row_at + col_at + step_number) % row_count
    local_ids = jnp.arange(local_rows, dtype=jnp.int32)

    def product(operand):
        return jnp.einsum(
            "aij,amjk->amik",
            operand[0],
            operand[1],
            precision=lax.Precision.HIGHEST,
            preferred_element_type=jnp.float32,
        )

    def one_slot(slot_index, running):
        inner_offset = start_class + col_count * (slot_index - slot_count)
        source = row_at + inner_offset
        layer_index = jnp.where(source % row_count == base_row, 0, 1)
        chosen = lax.dynamic_index_in_dim(right_tiles, layer_index, 0, keepdims=False)
        chosen = jnp.take(
            chosen, (local_ids + jnp.floor_divide(source, row_count)) % local_rows, axis=0
        )
        left_block = lax.dynamic_index_in_dim(left_blocks, slot_index, 1, keepdims=False)
        result = product((left_block, chosen))
        first_slot = slot_index + carry_over
        current = lax.dynamic_slice_in_dim(running, first_slot, slot_pairs, 1)
        return lax.dynamic_update_slice_in_dim(running, current + result, first_slot, 1)

    return lax.fori_loop(0, slot_pairs, one_slot, accumulated)


def per_device(upper, mask):
    row_count = lax.axis_size("row")
    col_count = lax.axis_size("col")
    digits = col_count.bit_length() - 1
    row_at = lax.axis_index("row")
    col_at = lax.axis_index("col")
    local_rows = upper.shape[0]
    slot_count = upper.shape[2]
    block_size = upper.shape[4]
    residue = row_at % col_count
    col_ids = jnp.arange(col_count, dtype=jnp.int32)
    row_ids = jnp.arange(row_count, dtype=jnp.int32)
    row_sources = (row_ids + col_at) % row_count
    col_sources = (col_ids - residue) % col_count
    present = mask.reshape(local_rows, slot_count).astype(jnp.float32)
    stored = (
        upper.reshape(local_rows, slot_count, block_size, block_size) * present[:, :, None, None]
    )
    diagonal = stored[:, 0] + jnp.swapaxes(stored[:, 0], -1, -2)
    upper_part = stored.at[:, 0].set(jnp.where(col_at == 0, diagonal, stored[:, 0]))

    def flip_out(value):
        return lax.all_to_all(value, "col", split_axis=0, concat_axis=0, tiled=True)

    def flip_back(value):
        return lax.all_to_all(value, "col", split_axis=0, concat_axis=0, tiled=True)

    flipped = route(stored, -col_ids % col_count, flip_out, flip_back)

    def rows_out(value):
        return lax.all_to_all(value, "row", split_axis=0, concat_axis=0, tiled=True)

    def rows_back(value):
        return lax.all_to_all(value, "row", split_axis=0, concat_axis=0, tiled=True)

    flipped = route(flipped, row_sources, rows_out, rows_back)
    partner = partner_2(flipped, "row", digits)
    lower_part = lower_blocks(flipped, partner, row_at, col_at, row_count, col_count)
    layout = jnp.concatenate([lower_part, upper_part], axis=1)

    def skew_out(value):
        return lax.all_to_all(value, "col", split_axis=0, concat_axis=0, tiled=True)

    def skew_back(value):
        return lax.all_to_all(value, "col", split_axis=0, concat_axis=0, tiled=True)

    skewed = route(layout, col_sources, skew_out, skew_back)

    def shear_out(value):
        return lax.all_to_all(value, "row", split_axis=0, concat_axis=0, tiled=True)

    def shear_back(value):
        return lax.all_to_all(value, "row", split_axis=0, concat_axis=0, tiled=True)

    skewed = route(skewed, row_sources, shear_out, shear_back)
    left_next = shifted(layout, "col", -1)
    paired = partner_2(skewed, "row", digits)
    first_tiles = jnp.stack([skewed, paired])
    moved_own, moved_pair = shifted((skewed, paired), "row", -1)
    second_tiles = jnp.stack([moved_own, moved_pair])
    accumulated = jnp.zeros((local_rows, 4 * slot_count, block_size, block_size), jnp.float32)
    accumulated = accumulate(
        accumulated, layout, first_tiles, 0, row_at, col_at, row_count, col_count
    )
    accumulated = accumulate(
        accumulated, left_next, second_tiles, 1, row_at, col_at, row_count, col_count
    )
    return accumulated.reshape(local_rows, 1, 4 * slot_count, 1, block_size, block_size)


def solution(mesh):
    in_specs = (P(None, "row", None, "col", None, None), P(None, "row", None, "col"))
    out_specs = P(None, "row", None, "col", None, None)
    return jax.shard_map(
        per_device, mesh=mesh, in_specs=in_specs, out_specs=out_specs, check_vma=False
    )
```

profile of v0, /device:TPU:7, one launch (start us, length us, event | category | flops | bytes accessed | tf_op | source)
XLA Modules:
  0.0 425.2 jit_solution(14075120420843760736)
XLA Ops:
  0.8 2.1 mul.80
  2.9 6.3 %all-to-all-start = ((f32[16,1,6144]{2,1,0:T(1,128)}), f32[16,1,6144]{2,1,0:T(1,128)S(1)}, u32[]{:S(2)}, u32[]{:S(2)}) async-start(f32[16,1,6144]{2,1,0:T(1,128)} %mul.80), calls=%async_computation | async-start | bytes 786432 | tf_op jit(solution)/shard_map/all_to_all | solution.py:117
  9.2 7.8 %all-to-all-done = f32[16,1,6144]{2,1,0:T(1,128)S(1)} async-done(((f32[16,1,6144]{2,1,0:T(1,128)}), f32[16,1,6144]{2,1,0:T(1,128)S(1)}, u32[]{:S(2)}, u32[]{:S(2)}) %all-to-all-start) | async-done | bytes 393248 | tf_op jit(solution)/shard_map/all_to_all | solution.py:117
  18.3 12.9 %all_to_all.69 = f32[16,1,6144]{2,1,0:T(1,128)} all-to-all(f32[16,1,6144]{2,1,0:T(1,128)S(1)} %copy.22), channel_id=1, replica_groups=mesh['row'=32,'col'=16] {'col'}, dimensions={0} | all-to-all | bytes 786432 | tf_op jit(solution)/shard_map/all_to_all | solution.py:120
  31.2 17.7 %all-to-all-start.2 = ((f32[32,1,3072]{2,1,0:T(1,128)}), f32[32,1,3072]{2,1,0:T(1,128)S(1)}, u32[]{:S(2)}, u32[]{:S(2)}) async-start(f32[32,1,3072]{2,1,0:T(1,128)} %bitcast.15), calls=%async_computation.2 | async-start | bytes 786432 | tf_op jit(solution)/shard_map/all_to_all | solution.py:125
  48.9 26.2 %all-to-all-done.2 = f32[32,1,3072]{2,1,0:T(1,128)S(1)} async-done(((f32[32,1,3072]{2,1,0:T(1,128)}), f32[32,1,3072]{2,1,0:T(1,128)S(1)}, u32[]{:S(2)}, u32[]{:S(2)}) %all-to-all-start.2) | async-done | bytes 393248 | tf_op jit(solution)/shard_map/all_to_all | solution.py:125
  77.2 5.5 %all-to-all-start.3 = ((f32[32,1,3072]{2,1,0:T(1,128)}), f32[32,1,3072]{2,1,0:T(1,128)S(1)}, u32[]{:S(2)}, u32[]{:S(2)}) async-start(f32[32,1,3072]{2,1,0:T(1,128)} %copy.24), calls=%async_computation.3 | async-start | bytes 786432 | tf_op jit(solution)/shard_map/all_to_all | solution.py:128
  83.0 24.3 %all-to-all-done.3 = f32[32,1,3072]{2,1,0:T(1,128)S(1)} async-done(((f32[32,1,3072]{2,1,0:T(1,128)}), f32[32,1,3072]{2,1,0:T(1,128)S(1)}, u32[]{:S(2)}, u32[]{:S(2)}) %all-to-all-start.3) | async-done | bytes 393248 | tf_op jit(solution)/shard_map/all_to_all | solution.py:128
  107.3 4.7 %collective-permute-start = (f32[1,6,128,128]{3,2,1,0:T(8,128)S(1)}, f32[1,6,128,128]{3,2,1,0:T(8,128)S(1)}, u32[]{:S(2)}, u32[]{:S(2)}) collective-permute-start(f32[1,6,128,128]{3,2,1,0:T(8,128)S(1)} %bitcast.123), channel_id=1, source_target_pairs={{0,256},{256,0},{16,272},{272,16},{32,288},{288,32},{48,304},{304,... | collective-permute-start | bytes 1179656 | tf_op jit(solution)/shard_map/ppermute | solution.py:14
  112.7 29.2 %collective-permute-done = f32[1,6,128,128]{3,2,1,0:T(8,128)S(1)} collective-permute-done((f32[1,6,128,128]{3,2,1,0:T(8,128)S(1)}, f32[1,6,128,128]{3,2,1,0:T(8,128)S(1)}, u32[]{:S(2)}, u32[]{:S(2)}) %collective-permute-start) | collective-permute-done | bytes 393248 | tf_op jit(solution)/shard_map/ppermute | solution.py:14
  144.9 2.3 copy.28
  147.2 10.1 %all-to-all-start.4 = ((f32[16,1,12288]{2,1,0:T(1,128)}), f32[16,1,12288]{2,1,0:T(1,128)S(1)}, u32[]{:S(2)}, u32[]{:S(2)}) async-start(f32[16,1,12288]{2,1,0:T(1,128)} %bitcast.33), calls=%async_computation.4 | async-start | bytes 1572864 | tf_op jit(solution)/shard_map/all_to_all | solution.py:136
  157.4 11.8 %all-to-all-done.4 = f32[16,1,12288]{2,1,0:T(1,128)S(1)} async-done(((f32[16,1,12288]{2,1,0:T(1,128)}), f32[16,1,12288]{2,1,0:T(1,128)S(1)}, u32[]{:S(2)}, u32[]{:S(2)}) %all-to-all-start.4) | async-done | bytes 786464 | tf_op jit(solution)/shard_map/all_to_all | solution.py:136
  171.4 16.7 %all_to_all.70 = f32[16,1,12288]{2,1,0:T(1,128)S(1)} all-to-all(f32[16,1,12288]{2,1,0:T(1,128)S(1)} %copy.30), channel_id=1, replica_groups=mesh['row'=32,'col'=16] {'col'}, dimensions={0} | all-to-all | bytes 1572864 | tf_op jit(solution)/shard_map/all_to_all | solution.py:139
  188.1 56.6 %all_to_all.71 = f32[32,1,6144]{2,1,0:T(1,128)S(1)} all-to-all(f32[32,1,6144]{2,1,0:T(1,128)S(1)} %bitcast.120), channel_id=1, replica_groups=mesh['row'=32,'col'=16] {'row'}, dimensions={0} | all-to-all | bytes 1572864 | tf_op jit(solution)/shard_map/all_to_all | solution.py:144
  246.7 48.9 %all_to_all.72 = f32[32,1,6144]{2,1,0:T(1,128)S(1)} all-to-all(f32[32,1,6144]{2,1,0:T(1,128)S(1)} %copy.32), channel_id=1, replica_groups=mesh['row'=32,'col'=16] {'row'}, dimensions={0} | all-to-all | bytes 1572864 | tf_op jit(solution)/shard_map/all_to_all | solution.py:147
  296.8 3.7 collective-permute-start.1
  300.6 2.7 collective-permute-start.4
  303.3 3.5 collective-permute-start.2
  307.0 63.4 %collective-permute-done.1 = f32[1,12,128,128]{2,3,1,0:T(8,128)} collective-permute-done((f32[1,12,128,128]{2,3,1,0:T(8,128)}, f32[1,12,128,128]{2,3,1,0:T(8,128)}, u32[]{:S(2)}, u32[]{:S(2)}) %collective-permute-start.1) | collective-permute-done | bytes 786464 | tf_op jit(solution)/shard_map/ppermute | solution.py:14
  371.7 8.4 %collective-permute-start.3 = (f32[1,12,128,128]{2,3,1,0:T(8,128)}, f32[1,12,128,128]{2,3,1,0:T(8,128)}, u32[]{:S(2)}, u32[]{:S(2)}) collective-permute-start(f32[1,12,128,128]{2,3,1,0:T(8,128)} %collective-permute-done.1), channel_id=1, source_target_pairs={{16,0},{32,16},{48,32},{64,48},{80,64},{96,80},{112,96},{128,112},... | collective-permute-start | bytes 2359304 | tf_op jit(solution)/shard_map/ppermute | solution.py:20
  380.3 20.3 %while.35 = (s32[]{:T(128)}, f32[1,24,128,128]{2,3,1,0:T(8,128)S(1)}, s32[]{:T(128)}, s32[]{:T(128)}, s32[]{:T(128)}, /*index=5*/s32[]{:T(128)}, f32[2,1,12,128,...) while((s32[]{:T(128)}, ...), condition=%wide.region_1.2_spmd, body=%wide.region_0.1_spmd.sunk | while | flops 302186528 | bytes 2425718 | solution.py:92
  380.3 1.6 fusion.42
  382.0 1.6 fusion.42
  383.7 1.6 fusion.42
  385.4 1.6 fusion.42
  387.1 1.6 fusion.42
  388.8 1.6 fusion.42
  390.5 1.6 fusion.42
  392.2 1.6 fusion.42
  393.9 1.6 fusion.42
  395.6 1.6 fusion.42
  397.3 1.6 fusion.42
  399.0 1.6 fusion.42
  403.5 20.1 %while.36 = (s32[]{:T(128)}, f32[1,24,128,128]{2,3,1,0:T(8,128)S(1)}, s32[]{:T(128)}, s32[]{:T(128)}, s32[]{:T(128)}, /*index=5*/s32[]{:T(128)}, f32[2,1,12,128,...) while((s32[]{:T(128)}, ...), condition=%wide.region_3.4_spmd, body=%wide.region_2.3_spmd.sunk | while | flops 302186528 | bytes 2425718 | solution.py:92
  403.6 1.6 fusion.45
  405.2 1.6 fusion.45
  406.9 1.6 fusion.45
  408.6 1.6 fusion.45
  410.3 1.6 fusion.45
  411.9 1.6 fusion.45
  413.6 1.6 fusion.45
  415.3 1.6 fusion.45
  417.0 1.6 fusion.45
  418.6 1.6 fusion.45
  420.3 1.6 fusion.45
  422.0 1.6 fusion.45
  423.6 1.6 copy.38
  (54 shorter events, 18.0 us)
Async XLA Ops:
  2.9 14.1 %all-to-all-start = ((f32[16,1,6144]{2,1,0:T(1,128)}), f32[16,1,6144]{2,1,0:T(1,128)S(1)}, u32[]{:S(2)}, u32[]{:S(2)}) async-start(f32[16,1,6144]{2,1,0:T(1,128)} %mul.80), calls=%async_computation | async-start | bytes 786432 | tf_op jit(solution)/shard_map/all_to_all | solution.py:117
  31.2 43.9 %all-to-all-start.2 = ((f32[32,1,3072]{2,1,0:T(1,128)}), f32[32,1,3072]{2,1,0:T(1,128)S(1)}, u32[]{:S(2)}, u32[]{:S(2)}) async-start(f32[32,1,3072]{2,1,0:T(1,128)} %bitcast.15), calls=%async_computation.2 | async-start | bytes 786432 | tf_op jit(solution)/shard_map/all_to_all | solution.py:125
  75.9 6.7 %copy-start = (f32[1,1,6,1,128,128]{5,4,3,2,1,0:T(8,128)S(1)}, f32[1,1,6,1,128,128]{5,4,3,2,1,0:T(8,128)}, u32[]{:S(2)}) copy-start(f32[1,1,6,1,128,128]{5,4,3,2,1,0:T(8,128)} %param.8) | copy-start | bytes 1179652
  77.2 30.1 %all-to-all-start.3 = ((f32[32,1,3072]{2,1,0:T(1,128)}), f32[32,1,3072]{2,1,0:T(1,128)S(1)}, u32[]{:S(2)}, u32[]{:S(2)}) async-start(f32[32,1,3072]{2,1,0:T(1,128)} %copy.24), calls=%async_computation.3 | async-start | bytes 786432 | tf_op jit(solution)/shard_map/all_to_all | solution.py:128
  107.3 34.6 %collective-permute-start = (f32[1,6,128,128]{3,2,1,0:T(8,128)S(1)}, f32[1,6,128,128]{3,2,1,0:T(8,128)S(1)}, u32[]{:S(2)}, u32[]{:S(2)}) collective-permute-start(f32[1,6,128,128]{3,2,1,0:T(8,128)S(1)} %bitcast.123), channel_id=1, source_target_pairs={{0,256},{256,0},{16,272},{272,16},{32,288},{288,32},{48,304},{304,... | collective-permute-start | bytes 1179656 | tf_op jit(solution)/shard_map/ppermute | solution.py:14
  142.7 1.2 copy-start.1
  147.2 22.0 %all-to-all-start.4 = ((f32[16,1,12288]{2,1,0:T(1,128)}), f32[16,1,12288]{2,1,0:T(1,128)S(1)}, u32[]{:S(2)}, u32[]{:S(2)}) async-start(f32[16,1,12288]{2,1,0:T(1,128)} %bitcast.33), calls=%async_computation.4 | async-start | bytes 1572864 | tf_op jit(solution)/shard_map/all_to_all | solution.py:136
  296.8 73.7 %collective-permute-start.1 = (f32[1,12,128,128]{2,3,1,0:T(8,128)}, f32[1,12,128,128]{2,3,1,0:T(8,128)}, u32[]{:S(2)}, u32[]{:S(2)}) collective-permute-start(f32[1,12,128,128]{2,3,1,0:T(8,128)} %copy.33), channel_id=1, source_target_pairs={{0,256},{256,0},{16,272},{272,16},{32,288},{288,32},{48,304},{304,... | collective-permute-start | bytes 2359304 | tf_op jit(solution)/shard_map/ppermute | solution.py:14
  300.6 102.9 %collective-permute-start.4 = (f32[1,12,128,128]{2,3,1,0:T(8,128)}, f32[1,12,128,128]{2,3,1,0:T(8,128)}, u32[]{:S(2)}, u32[]{:S(2)}) collective-permute-start(f32[1,12,128,128]{2,3,1,0:T(8,128)} %pad_maximum_fusion.3), channel_id=1, source_target_pairs={{1,0},{2,1},{3,2},{4,3},{5,4},{6,5},{7,6},{8,7},{9,8},{10,9},{11,1... | collective-permute-start | bytes 2359304 | tf_op jit(solution)/shard_map/ppermute | solution.py:20
  303.3 97.3 %collective-permute-start.2 = (f32[1,12,128,128]{2,3,1,0:T(8,128)}, f32[1,12,128,128]{2,3,1,0:T(8,128)}, u32[]{:S(2)}, u32[]{:S(2)}) collective-permute-start(f32[1,12,128,128]{2,3,1,0:T(8,128)} %copy.33), channel_id=1, source_target_pairs={{16,0},{32,16},{48,32},{64,48},{80,64},{96,80},{112,96},{128,112},... | collective-permute-start | bytes 2359304 | tf_op jit(solution)/shard_map/ppermute | solution.py:20
  371.7 30.3 %collective-permute-start.3 = (f32[1,12,128,128]{2,3,1,0:T(8,128)}, f32[1,12,128,128]{2,3,1,0:T(8,128)}, u32[]{:S(2)}, u32[]{:S(2)}) collective-permute-start(f32[1,12,128,128]{2,3,1,0:T(8,128)} %collective-permute-done.1), channel_id=1, source_target_pairs={{16,0},{32,16},{48,32},{64,48},{80,64},{96,80},{112,96},{128,112},... | collective-permute-start | bytes 2359304 | tf_op jit(solution)/shard_map/ppermute | solution.py:20
where the time goes:
time: 427 us; the launch traced here: 425 us
  waiting for transfers between devices  164 us (38%)
  blocking collectives  135 us (32%)
  starting transfers between devices  62.5 us (15%)
  matrix products  39 us (9%)
  local copies, waits for them, and re-layouts  14.8 us (3%)
  other arithmetic  7.81 us (2%)
    ppermute x2, waiting for transfers between devices, partner_2(): return lax.ppermute(block, axis, route)  92.6 us
    all_to_all x1, blocking collectives, shear_out(): return lax.all_to_all(value, 'row', split_axis=0, concat_axis=0, tiled=True)  56.6 us
    all_to_all x1, blocking collectives, shear_back(): return lax.all_to_all(value, 'row', split_axis=0, concat_axis=0, tiled=True)  48.9 us
    dot_general x24, matrix products, product(): jnp.einsum('aij,amjk->amik', operand[0], operand[1], precision=lax.Precis...  39 us
    all_to_all x1, waiting for transfers between devices, rows_out(): return lax.all_to_all(value, 'row', split_axis=0, concat_axis=0, tiled=True)  26.2 us
    all_to_all x1, waiting for transfers between devices, rows_back(): return lax.all_to_all(value, 'row', split_axis=0, concat_axis=0, tiled=True)  24.3 us
    all_to_all x1, starting transfers between devices, rows_out(): return lax.all_to_all(value, 'row', split_axis=0, concat_axis=0, tiled=True)  17.7 us
    all_to_all x1, blocking collectives, skew_back(): return lax.all_to_all(value, 'col', split_axis=0, concat_axis=0, tiled=True)  16.7 us
  transfers between devices with their start and end apart: 9, of which 7 were waited for; matrix products, arithmetic and copies ran while one was open for 6% of the time, Pallas kernels for 0%

commit v1 on v0

v1 whole, which is shorter than its diff:
```python
import jax
import jax.numpy as jnp
from jax import lax
from jax.experimental import pallas as pl
from jax.experimental.pallas import tpu as pltpu
from jax.sharding import PartitionSpec as P

MESH_AXES = ("row", "col")


def permute(value, row_count, col_count, source_of):
    pairs = []
    for p in range(row_count):
        for q in range(col_count):
            source_row, source_col = source_of(p, q)
            source = source_row % row_count * col_count + source_col % col_count
            pairs.append((source, p * col_count + q))
    return lax.ppermute(value, MESH_AXES, pairs)


def split(value):
    high = value.astype(jnp.bfloat16)
    return high, (value - high.astype(jnp.float32)).astype(jnp.bfloat16)


def band_kernel(mirrored, scalars, mirror_a, mirror_b, stored, right_a, right_b, total, out, left_high, left_low, tiles_high, tiles_low):
    half = mirror_a.shape[0]
    size = stored.shape[1]
    slots = stored.shape[0]
    left_zero = scalars[0]
    flip = scalars[1]
    right_zero = scalars[2]
    first = scalars[3]

    def put_left(slot, block):
        high, low = split(block)
        at = (pl.ds(slot // 2 * size, size), pl.ds(slot % 2 * size, size))
        left_high[at] = high
        left_low[at] = low

    for pair in range(half):
        pick = jnp.minimum(half - 1 - pair + left_zero, half - 1)
        block = mirror_a[pick].T
        if pair == 0:
            block = block * (1 - left_zero).astype(jnp.float32)
        put_left(2 * pair, block)
        put_left(2 * pair + 1, mirror_b[half - 1 - pair].T)
    for slot in range(slots):
        block = stored[slot]
        if slot == 0:
            block = block + block.T * left_zero.astype(jnp.float32)
        put_left(slots + slot, block)

    def right_block(layer, slot):
        swapped = flip if layer == 0 else 1 - flip
        if mirrored:
            stored_slot = slots - 1 - slot
            swapped = swapped if stored_slot % 2 == 0 else 1 - swapped
            both = jnp.where(swapped == 0, right_a[stored_slot], right_b[stored_slot])
            if stored_slot == 0:
                both = both * (1 - right_zero).astype(jnp.float32)
            return both.T
        both = jnp.where(swapped == 0, right_a[slot], right_b[slot])
        if slot == 0:
            both = both + both.T * right_zero.astype(jnp.float32)
        return both

    zero = jnp.zeros((size, size), jnp.bfloat16)
    tile_count = slots // 2 + 1
    for tile in range(tile_count):
        for layer in range(2):
            for column in range(2):
                slot = 2 * tile + column - layer
                at = (tile, pl.ds(layer * size, size), pl.ds(column * size, size))
                if 0 <= slot < slots:
                    high, low = split(right_block(layer, slot))
                    tiles_high[at] = high
                    tiles_low[at] = low
                else:
                    tiles_high[at] = zero
                    tiles_low[at] = zero

    out[...] = total[...]
    left_pairs = left_high.shape[0] // size
    for tile in range(tile_count):
        high = tiles_high[tile]
        low = tiles_low[tile]
        for pair in range(left_pairs):
            rows = pl.ds(pair * size, size)
            part_high = left_high[rows, :]
            part = jnp.dot(part_high, high, preferred_element_type=jnp.float32)
            part = part + jnp.dot(part_high, low, preferred_element_type=jnp.float32)
            part = part + jnp.dot(left_low[rows, :], high, preferred_element_type=jnp.float32)
            at = 2 * (tile + pair) + first
            out[at] += part[:, :size]
            if tile < tile_count - 1:
                out[at + 1] += part[:, size:]


def add_products(total, mirrored, scalars, mirror_a, mirror_b, stored, right_a, right_b):
    slots, size, _ = stored.shape
    vmem = pl.BlockSpec(memory_space=pltpu.VMEM)

    def kernel(*refs):
        band_kernel(mirrored, *refs)

    return pl.pallas_call(
        kernel,
        out_shape=jax.ShapeDtypeStruct(total.shape, jnp.float32),
        in_specs=[pl.BlockSpec(memory_space=pltpu.SMEM)] + [vmem] * 6,
        out_specs=vmem,
        scratch_shapes=[
            pltpu.VMEM((slots * size, 2 * size), jnp.bfloat16),
            pltpu.VMEM((slots * size, 2 * size), jnp.bfloat16),
            pltpu.VMEM((slots // 2 + 1, 2 * size, 2 * size), jnp.bfloat16),
            pltpu.VMEM((slots // 2 + 1, 2 * size, 2 * size), jnp.bfloat16),
        ],
        compiler_params=pltpu.CompilerParams(vmem_limit_bytes=24 * 1024 * 1024),
        cost_estimate=pl.CostEstimate(flops=4 * slots * slots * size**3 * 3, bytes_accessed=4 * 1024 * 1024, transcendentals=0),
    )(scalars, mirror_a, mirror_b, stored, right_a, right_b, total)


def per_device(upper, mask):
    row_count = lax.axis_size("row")
    col_count = lax.axis_size("col")
    p = lax.axis_index("row")
    q = lax.axis_index("col")
    slots = upper.shape[2]
    size = upper.shape[4]
    b = p % col_count

    def send(value, source_of):
        return permute(value, row_count, col_count, source_of)

    present = mask.reshape(slots).astype(jnp.float32)
    stored = upper.reshape(slots, size, size) * present[:, None, None]

    by_parity = stored.reshape(slots // 2, 2, size, size)
    even, odd = by_parity[:, 0], by_parity[:, 1]
    at_zero = q == 0
    for_left = jnp.concatenate([jnp.where(at_zero, even, odd), jnp.where(at_zero, odd, even)])
    via_left = send(for_left, lambda p, q: (p, q - 2 * p))
    via_upper = send(stored, lambda p, q: (p, p - q))
    via_lower = send(stored, lambda p, q: (p, q - p))
    stored_next = send(stored, lambda p, q: (p, q + 1))

    mirror = []
    upper_right = []
    lower_right = []
    for layer in range(2):
        shift = layer * col_count

        def from_sum(p, q):
            return (p + q + shift, 2 * p + q)

        half = via_left[layer * (slots // 2) : (layer + 1) * (slots // 2)]
        mirror.append(send(half, from_sum))
        upper_right.append(send(via_upper, from_sum))
    for layer in range(2):
        shift = layer * col_count

        def from_col(p, q):
            return (q + p // col_count * col_count + shift, p + q)

        lower_right.append(send(via_lower, from_col))

    def up_one(value):
        return send(value, lambda p, q: (p + 1, q))

    def along_one(value):
        return send(value, lambda p, q: (p, q + 1))

    mirror_next = [along_one(value) for value in mirror]
    upper_next = [up_one(value) for value in upper_right]
    lower_next = [up_one(value) for value in lower_right]

    def scalars(step, mirrored):
        start = (q + step) % col_count
        right = (-b - step) % col_count
        target = (q - b) % col_count
        carry = (start + right - target) // col_count
        left_zero = (start == 0).astype(jnp.int32)
        right_zero = (right == 0).astype(jnp.int32)
        flip = (q + step >= col_count).astype(jnp.int32)
        first = carry + (right_zero if mirrored else slots)
        return jnp.stack([left_zero, flip, right_zero, first]).astype(jnp.int32)

    total = jnp.zeros((4 * slots, size, size), jnp.float32)
    total = add_products(total, False, scalars(0, False), *mirror, stored, *upper_right)
    total = add_products(total, False, scalars(1, False), *mirror_next, stored_next, *upper_next)
    total = add_products(total, True, scalars(0, True), *mirror, stored, *lower_right)
    total = add_products(total, True, scalars(1, True), *mirror_next, stored_next, *lower_next)
    return total.reshape(1, 1, 4 * slots, 1, size, size)


def solution(mesh):
    in_specs = (P(None, "row", None, "col", None, None), P(None, "row", None, "col"))
    out_specs = P(None, "row", None, "col", None, None)
    return jax.shard_map(
        per_device, mesh=mesh, in_specs=in_specs, out_specs=out_specs, check_vma=False
    )
```

time: 427 us -> 175 us (0.41)
  the two profiles are of different devices: /device:TPU:7 before, /device:TPU:16 now
where the time goes in v1:
time: 175 us
  starting transfers between devices  126 us (72%)
  waiting for transfers between devices  35.9 us (21%)
  Pallas kernels  10 us (6%)
  other arithmetic  2.3 us (1%)
    ppermute x16, starting transfers between devices, permute(): return lax.ppermute(value, MESH_AXES, pairs)  126 us
    ppermute x16, waiting for transfers between devices, permute(): return lax.ppermute(value, MESH_AXES, pairs)  35.9 us
    pallas_call x4, Pallas kernels, add_products(): pl.pallas_call(kernel, out_shape=jax.ShapeDtypeStruct(total.shape, jnp.fl...  10 us
  transfers between devices with their start and end apart: 16, of which 5 were waited for; matrix products, arithmetic and copies ran while one was open for 0% of the time, Pallas kernels for 4%

profile of v1, /device:TPU:16, one launch (start us, length us, event | category | flops | bytes accessed | tf_op | source)
XLA Modules:
  0.0 174.6 jit_solution(2605987141919928023)
XLA Ops:
  0.0 0.7 convert_reduce_fusion
  0.7 0.1 convert_element_type.32
  0.8 0.1 copy.5
  0.9 1.1 copy_multiply_fusion
  2.1 0.7 collective-permute-start
  2.8 0.0 copy-done.1
  2.8 0.0 copy-done
  2.8 0.1 bitcast_multiply_fusion.refs_3_
  2.9 3.4 %collective-permute-start.11 = (f32[6,128,128]{2,1,0:T(8,128)S(1)}, f32[6,128,128]{2,1,0:T(8,128)}, u32[]{:S(2)}, u32[]{:S(2)}) collective-permute-start(f32[6,128,128]{2,1,0:T(8,128)S(1)} %bitcast_multiply_fusion.refs_3_), channel_id=1, source_target_pairs={{0,0},{15,1},{14,2},{13,3},{12,4},{11,5},{10,6},{9,7},{8,8},{7,9},... | collective-permute-start | bytes 1179656 | tf_op jit(solution)/shard_map/ppermute | solution.py:18
  6.3 2.5 %collective-permute-start.5 = (f32[6,128,128]{2,1,0:T(8,128)S(1)}, f32[6,128,128]{2,1,0:T(8,128)S(1)}, u32[]{:S(2)}, u32[]{:S(2)}) collective-permute-start(f32[6,128,128]{2,1,0:T(8,128)S(1)} %bitcast_multiply_fusion.refs_3_), channel_id=1, source_target_pairs={{1,0},{2,1},{3,2},{4,3},{5,4},{6,5},{7,6},{8,7},{9,8},{10,9},{11,1... | collective-permute-start | bytes 1179656 | tf_op jit(solution)/shard_map/ppermute | solution.py:18
  8.9 0.7 collective-permute-start.6
  9.6 0.0 collective-permute-done
  9.6 22.2 %collective-permute-start.1 = (f32[3,128,128]{2,1,0:T(8,128)S(1)}, f32[3,128,128]{2,1,0:T(8,128)S(1)}, u32[]{:S(2)}, u32[]{:S(2)}) collective-permute-start(f32[3,128,128]{2,1,0:T(8,128)S(1)} %get-tuple-element.10), channel_id=1, source_target_pairs={{0,0},{17,1},{34,2},{51,3},{68,4},{85,5},{102,6},{119,7},{136,8},{... | collective-permute-start | bytes 589832 | tf_op jit(solution)/shard_map/ppermute | solution.py:18
  31.8 1.9 %collective-permute-start.3 = (f32[3,128,128]{2,1,0:T(8,128)S(1)}, f32[3,128,128]{2,1,0:T(8,128)S(1)}, u32[]{:S(2)}, u32[]{:S(2)}) collective-permute-start(f32[3,128,128]{2,1,0:T(8,128)S(1)} %get-tuple-element.9), channel_id=1, source_target_pairs={{256,0},{273,1},{290,2},{307,3},{324,4},{341,5},{358,6},{375,7},{3... | collective-permute-start | bytes 589832 | tf_op jit(solution)/shard_map/ppermute | solution.py:18
  33.7 0.0 collective-permute-done.11
  33.7 6.0 %collective-permute-start.12 = (f32[6,128,128]{2,1,0:T(8,128)}, f32[6,128,128]{2,1,0:T(8,128)S(1)}, u32[]{:S(2)}, u32[]{:S(2)}) collective-permute-start(f32[6,128,128]{2,1,0:T(8,128)} %collective-permute-done.11), channel_id=1, source_target_pairs={{0,0},{17,1},{34,2},{51,3},{68,4},{85,5},{102,6},{119,7},{136,8},{... | collective-permute-start | bytes 1179656 | tf_op jit(solution)/shard_map/ppermute | solution.py:18
  39.7 0.0 collective-permute-done.5.refs_3_
  39.8 1.9 %collective-permute-start.14 = (f32[6,128,128]{2,1,0:T(8,128)}, f32[6,128,128]{2,1,0:T(8,128)S(1)}, u32[]{:S(2)}, u32[]{:S(2)}) collective-permute-start(f32[6,128,128]{2,1,0:T(8,128)} %collective-permute-done.11), channel_id=1, source_target_pairs={{256,0},{273,1},{290,2},{307,3},{324,4},{341,5},{358,6},{375,7},{3... | collective-permute-start | bytes 1179656 | tf_op jit(solution)/shard_map/ppermute | solution.py:18
  41.8 0.0 collective-permute-done.6
  41.8 5.6 %collective-permute-start.7 = (f32[6,128,128]{2,1,0:T(8,128)S(1)}, f32[6,128,128]{2,1,0:T(8,128)S(1)}, u32[]{:S(2)}, u32[]{:S(2)}) collective-permute-start(f32[6,128,128]{2,1,0:T(8,128)S(1)} %collective-permute-done.6), channel_id=1, source_target_pairs={{0,0},{17,1},{34,2},{51,3},{68,4},{85,5},{102,6},{119,7},{136,8},{... | collective-permute-start | bytes 1179656 | tf_op jit(solution)/shard_map/ppermute | solution.py:18
  47.4 0.0 collective-permute-done.1.refs_1_
  47.4 16.5 %collective-permute-start.9 = (f32[6,128,128]{2,1,0:T(8,128)S(1)}, f32[6,128,128]{2,1,0:T(8,128)S(1)}, u32[]{:S(2)}, u32[]{:S(2)}) collective-permute-start(f32[6,128,128]{2,1,0:T(8,128)S(1)} %collective-permute-done.6), channel_id=1, source_target_pairs={{256,0},{273,1},{290,2},{307,3},{324,4},{341,5},{358,6},{375,7},{3... | collective-permute-start | bytes 1179656 | tf_op jit(solution)/shard_map/ppermute | solution.py:18
  63.9 0.1 pad_add_fusion.5
  64.0 0.0 collective-permute-done.3.refs_2_
  64.0 11.9 %collective-permute-start.2 = (f32[3,128,128]{2,1,0:T(8,128)S(1)}, f32[3,128,128]{2,1,0:T(8,128)S(1)}, u32[]{:S(2)}, u32[]{:S(2)}) collective-permute-start(f32[3,128,128]{2,1,0:T(8,128)S(1)} %collective-permute-done.1.refs_1_), channel_id=1, source_target_pairs={{1,0},{2,1},{3,2},{4,3},{5,4},{6,5},{7,6},{8,7},{9,8},{10,9},{11,1... | collective-permute-start | bytes 589832 | tf_op jit(solution)/shard_map/ppermute | solution.py:18
  75.9 0.1 pad_add_fusion.2.refs_0_
  75.9 0.0 collective-permute-done.12.refs_4_
  75.9 6.0 %collective-permute-start.13 = (f32[6,128,128]{2,1,0:T(8,128)S(1)}, f32[6,128,128]{2,1,0:T(8,128)S(1)}, u32[]{:S(2)}, u32[]{:S(2)}) collective-permute-start(f32[6,128,128]{2,1,0:T(8,128)S(1)} %collective-permute-done.12.refs_4_), channel_id=1, source_target_pairs={{16,0},{17,1},{18,2},{19,3},{20,4},{21,5},{22,6},{23,7},{24,8},{25... | collective-permute-start | bytes 1179656 | tf_op jit(solution)/shard_map/ppermute | solution.py:18
  81.9 0.0 collective-permute-done.14.refs_5_
  81.9 34.7 %collective-permute-start.15 = (f32[6,128,128]{2,1,0:T(8,128)S(1)}, f32[6,128,128]{2,1,0:T(8,128)S(1)}, u32[]{:S(2)}, u32[]{:S(2)}) collective-permute-start(f32[6,128,128]{2,1,0:T(8,128)S(1)} %collective-permute-done.14.refs_5_), channel_id=1, source_target_pairs={{16,0},{17,1},{18,2},{19,3},{20,4},{21,5},{22,6},{23,7},{24,8},{25... | collective-permute-start | bytes 1179656 | tf_op jit(solution)/shard_map/ppermute | solution.py:18
  116.7 0.1 pad_add_fusion.4
  116.8 0.0 collective-permute-done.2.refs_1_
  116.8 7.8 %collective-permute-start.4 = (f32[3,128,128]{2,1,0:T(8,128)S(1)}, f32[3,128,128]{2,1,0:T(8,128)S(1)}, u32[]{:S(2)}, u32[]{:S(2)}) collective-permute-start(f32[3,128,128]{2,1,0:T(8,128)S(1)} %collective-permute-done.3.refs_2_), channel_id=1, source_target_pairs={{1,0},{2,1},{3,2},{4,3},{5,4},{6,5},{7,6},{8,7},{9,8},{10,9},{11,1... | collective-permute-start | bytes 589832 | tf_op jit(solution)/shard_map/ppermute | solution.py:18
  124.6 13.3 %collective-permute-done.9.refs_5_ = f32[6,128,128]{2,1,0:T(8,128)S(1)} collective-permute-done((f32[6,128,128]{2,1,0:T(8,128)S(1)}, f32[6,128,128]{2,1,0:T(8,128)S(1)}, u32[]{:S(2)}, u32[]{:S(2)}) %collective-permute-start.9) | collective-permute-done | bytes 393248 | tf_op jit(solution)/shard_map/ppermute | solution.py:18
  137.9 1.9 %collective-permute-start.10 = (f32[6,128,128]{2,1,0:T(8,128)S(1)}, f32[6,128,128]{2,1,0:T(8,128)S(1)}, u32[]{:S(2)}, u32[]{:S(2)}) collective-permute-start(f32[6,128,128]{2,1,0:T(8,128)S(1)} %collective-permute-done.9.refs_5_), channel_id=1, source_target_pairs={{16,0},{17,1},{18,2},{19,3},{20,4},{21,5},{22,6},{23,7},{24,8},{25... | collective-permute-start | bytes 1179656 | tf_op jit(solution)/shard_map/ppermute | solution.py:18
  139.8 0.0 collective-permute-done.7.refs_4_
  139.8 1.9 %collective-permute-start.8 = (f32[6,128,128]{2,1,0:T(8,128)S(1)}, f32[6,128,128]{2,1,0:T(8,128)S(1)}, u32[]{:S(2)}, u32[]{:S(2)}) collective-permute-start(f32[6,128,128]{2,1,0:T(8,128)S(1)} %collective-permute-done.7.refs_4_), channel_id=1, source_target_pairs={{16,0},{17,1},{18,2},{19,3},{20,4},{21,5},{22,6},{23,7},{24,8},{25... | collective-permute-start | bytes 1179656 | tf_op jit(solution)/shard_map/ppermute | solution.py:18
  141.8 0.1 pad_add_fusion.refs_0_
  141.8 0.2 broadcast_in_dim.4.refs_6_
  142.0 2.2 %shard_map.28.refs_6_ = f32[24,128,128]{2,1,0:T(8,128)S(1)} custom-call(s32[4]{0:T(128)S(1)} %get-tuple-element.5.refs_0_, f32[3,128,128]{2,1,0:T(8,128)S(1)} %collective-permute-done.1.refs_1_, f32[3,128,128]{2,1,0:T(8,128)S(1)} %collective-permute-done.3.refs_2_, f32[6,128,128]{2,1,0:T(8,128)S(1)} %bitcast_multiply_fusion.refs_3_, ...), custom_call_target="tpu_custom_call" | custom-call | flops 905969664 | bytes 4194304 | tf_op jit(solution)/shard_map/pallas_call | solution.py:107
  144.2 0.0 collective-permute-done.4.refs_2_
  144.2 2.3 %collective-permute-done.13.refs_4_ = f32[6,128,128]{2,1,0:T(8,128)S(1)} collective-permute-done((f32[6,128,128]{2,1,0:T(8,128)S(1)}, f32[6,128,128]{2,1,0:T(8,128)S(1)}, u32[]{:S(2)}, u32[]{:S(2)}) %collective-permute-start.13) | collective-permute-done | bytes 393248 | tf_op jit(solution)/shard_map/ppermute | solution.py:18
  146.5 8.4 %collective-permute-done.15.refs_5_ = f32[6,128,128]{2,1,0:T(8,128)S(1)} collective-permute-done((f32[6,128,128]{2,1,0:T(8,128)S(1)}, f32[6,128,128]{2,1,0:T(8,128)S(1)}, u32[]{:S(2)}, u32[]{:S(2)}) %collective-permute-start.15) | collective-permute-done | bytes 393248 | tf_op jit(solution)/shard_map/ppermute | solution.py:18
  154.9 2.2 %shard_map.29.refs_6_ = f32[24,128,128]{2,1,0:T(8,128)S(1)} custom-call(s32[4]{0:T(128)S(1)} %get-tuple-element.7.refs_0_, f32[3,128,128]{2,1,0:T(8,128)S(1)} %collective-permute-done.2.refs_1_, f32[3,128,128]{2,1,0:T(8,128)S(1)} %collective-permute-done.4.refs_2_, f32[6,128,128]{2,1,0:T(8,128)S(1)} %collective-permute-done.5.refs_3_, ...), custom_call_target="tpu_custom_call" | custom-call | flops 905969664 | bytes 4194304 | tf_op jit(solution)/shard_map/pallas_call | solution.py:107
  157.1 2.2 %shard_map.30.refs_6_ = f32[24,128,128]{2,1,0:T(8,128)S(1)} custom-call(s32[4]{0:T(128)S(1)} %pad_add_fusion.2.refs_0_, f32[3,128,128]{2,1,0:T(8,128)S(1)} %collective-permute-done.1.refs_1_, f32[3,128,128]{2,1,0:T(8,128)S(1)} %collective-permute-done.3.refs_2_, f32[6,128,128]{2,1,0:T(8,128)S(1)} %bitcast_multiply_fusion.refs_3_, ...), custom_call_target="tpu_custom_call" | custom-call | flops 905969664 | bytes 4194304 | tf_op jit(solution)/shard_map/pallas_call | solution.py:107
  159.4 4.0 %collective-permute-done.10.refs_5_ = f32[6,128,128]{2,1,0:T(8,128)S(1)} collective-permute-done((f32[6,128,128]{2,1,0:T(8,128)S(1)}, f32[6,128,128]{2,1,0:T(8,128)S(1)}, u32[]{:S(2)}, u32[]{:S(2)}) %collective-permute-start.10) | collective-permute-done | bytes 393248 | tf_op jit(solution)/shard_map/ppermute | solution.py:18
  163.3 7.9 %collective-permute-done.8.refs_4_ = f32[6,128,128]{2,1,0:T(8,128)S(1)} collective-permute-done((f32[6,128,128]{2,1,0:T(8,128)S(1)}, f32[6,128,128]{2,1,0:T(8,128)S(1)}, u32[]{:S(2)}, u32[]{:S(2)}) %collective-permute-start.8) | collective-permute-done | bytes 393248 | tf_op jit(solution)/shard_map/ppermute | solution.py:18
  171.3 3.4 %shard_map.31 = f32[24,128,128]{2,1,0:T(8,128)} custom-call(s32[4]{0:T(128)S(1)} %pad_add_fusion.refs_0_, f32[3,128,128]{2,1,0:T(8,128)S(1)} %collective-permute-done.2.refs_1_, f32[3,128,128]{2,1,0:T(8,128)S(1)} %collective-permute-done.4.refs_2_, f32[6,128,128]{2,1,0:T(8,128)S(1)} %collective-permute-done.5.refs_3_, ...), custom_call_target="tpu_custom_call" | custom-call | flops 905969664 | bytes 4194304 | tf_op jit(solution)/shard_map/pallas_call | solution.py:107
  (6 shorter events, 0.1 us)
Async XLA Ops:
  0.0 2.8 %copy-start.1 = (s32[1,1,6,1]{2,3,1,0:T(1,128)S(1)}, s32[1,1,6,1]{2,3,1,0:T(1,128)}, u32[]{:S(2)}) copy-start(s32[1,1,6,1]{2,3,1,0:T(1,128)} %param.3) | copy-start | bytes 76
  0.0 2.8 %copy-start = (f32[1,1,6,1,128,128]{5,4,3,2,1,0:T(8,128)S(1)}, f32[1,1,6,1,128,128]{5,4,3,2,1,0:T(8,128)}, u32[]{:S(2)}) copy-start(f32[1,1,6,1,128,128]{5,4,3,2,1,0:T(8,128)} %param.2) | copy-start | bytes 1179652
  2.1 7.5 %collective-permute-start = (f32[6,128,128]{2,1,0:T(8,128)S(1)}, f32[6,128,128]{2,1,0:T(8,128)S(1)}, u32[]{:S(2)}, u32[]{:S(2)}) collective-permute-start(f32[6,128,128]{2,1,0:T(8,128)S(1)} %pad_maximum_fusion), channel_id=1, source_target_pairs={{0,0},{1,1},{2,2},{3,3},{4,4},{5,5},{6,6},{7,7},{8,8},{9,9},{10,10... | collective-permute-start | bytes 1179656 | tf_op jit(solution)/shard_map/ppermute | solution.py:18
  2.9 30.8 %collective-permute-start.11 = (f32[6,128,128]{2,1,0:T(8,128)S(1)}, f32[6,128,128]{2,1,0:T(8,128)}, u32[]{:S(2)}, u32[]{:S(2)}) collective-permute-start(f32[6,128,128]{2,1,0:T(8,128)S(1)} %bitcast_multiply_fusion.refs_3_), channel_id=1, source_target_pairs={{0,0},{15,1},{14,2},{13,3},{12,4},{11,5},{10,6},{9,7},{8,8},{7,9},... | collective-permute-start | bytes 1179656 | tf_op jit(solution)/shard_map/ppermute | solution.py:18
  6.3 33.4 %collective-permute-start.5 = (f32[6,128,128]{2,1,0:T(8,128)S(1)}, f32[6,128,128]{2,1,0:T(8,128)S(1)}, u32[]{:S(2)}, u32[]{:S(2)}) collective-permute-start(f32[6,128,128]{2,1,0:T(8,128)S(1)} %bitcast_multiply_fusion.refs_3_), channel_id=1, source_target_pairs={{1,0},{2,1},{3,2},{4,3},{5,4},{6,5},{7,6},{8,7},{9,8},{10,9},{11,1... | collective-permute-start | bytes 1179656 | tf_op jit(solution)/shard_map/ppermute | solution.py:18
  8.9 32.9 %collective-permute-start.6 = (f32[6,128,128]{2,1,0:T(8,128)S(1)}, f32[6,128,128]{2,1,0:T(8,128)S(1)}, u32[]{:S(2)}, u32[]{:S(2)}) collective-permute-start(f32[6,128,128]{2,1,0:T(8,128)S(1)} %bitcast_multiply_fusion.refs_3_), channel_id=1, source_target_pairs={{0,0},{1,1},{2,2},{3,3},{4,4},{5,5},{6,6},{7,7},{8,8},{9,9},{10,10... | collective-permute-start | bytes 1179656 | tf_op jit(solution)/shard_map/ppermute | solution.py:18
  9.6 37.8 %collective-permute-start.1 = (f32[3,128,128]{2,1,0:T(8,128)S(1)}, f32[3,128,128]{2,1,0:T(8,128)S(1)}, u32[]{:S(2)}, u32[]{:S(2)}) collective-permute-start(f32[3,128,128]{2,1,0:T(8,128)S(1)} %get-tuple-element.10), channel_id=1, source_target_pairs={{0,0},{17,1},{34,2},{51,3},{68,4},{85,5},{102,6},{119,7},{136,8},{... | collective-permute-start | bytes 589832 | tf_op jit(solution)/shard_map/ppermute | solution.py:18
  31.8 32.2 %collective-permute-start.3 = (f32[3,128,128]{2,1,0:T(8,128)S(1)}, f32[3,128,128]{2,1,0:T(8,128)S(1)}, u32[]{:S(2)}, u32[]{:S(2)}) collective-permute-start(f32[3,128,128]{2,1,0:T(8,128)S(1)} %get-tuple-element.9), channel_id=1, source_target_pairs={{256,0},{273,1},{290,2},{307,3},{324,4},{341,5},{358,6},{375,7},{3... | collective-permute-start | bytes 589832 | tf_op jit(solution)/shard_map/ppermute | solution.py:18
  33.7 42.2 %collective-permute-start.12 = (f32[6,128,128]{2,1,0:T(8,128)}, f32[6,128,128]{2,1,0:T(8,128)S(1)}, u32[]{:S(2)}, u32[]{:S(2)}) collective-permute-start(f32[6,128,128]{2,1,0:T(8,128)} %collective-permute-done.11), channel_id=1, source_target_pairs={{0,0},{17,1},{34,2},{51,3},{68,4},{85,5},{102,6},{119,7},{136,8},{... | collective-permute-start | bytes 1179656 | tf_op jit(solution)/shard_map/ppermute | solution.py:18
  39.8 42.2 %collective-permute-start.14 = (f32[6,128,128]{2,1,0:T(8,128)}, f32[6,128,128]{2,1,0:T(8,128)S(1)}, u32[]{:S(2)}, u32[]{:S(2)}) collective-permute-start(f32[6,128,128]{2,1,0:T(8,128)} %collective-permute-done.11), channel_id=1, source_target_pairs={{256,0},{273,1},{290,2},{307,3},{324,4},{341,5},{358,6},{375,7},{3... | collective-permute-start | bytes 1179656 | tf_op jit(solution)/shard_map/ppermute | solution.py:18
  41.8 98.1 %collective-permute-start.7 = (f32[6,128,128]{2,1,0:T(8,128)S(1)}, f32[6,128,128]{2,1,0:T(8,128)S(1)}, u32[]{:S(2)}, u32[]{:S(2)}) collective-permute-start(f32[6,128,128]{2,1,0:T(8,128)S(1)} %collective-permute-done.6), channel_id=1, source_target_pairs={{0,0},{17,1},{34,2},{51,3},{68,4},{85,5},{102,6},{119,7},{136,8},{... | collective-permute-start | bytes 1179656 | tf_op jit(solution)/shard_map/ppermute | solution.py:18
  47.4 90.5 %collective-permute-start.9 = (f32[6,128,128]{2,1,0:T(8,128)S(1)}, f32[6,128,128]{2,1,0:T(8,128)S(1)}, u32[]{:S(2)}, u32[]{:S(2)}) collective-permute-start(f32[6,128,128]{2,1,0:T(8,128)S(1)} %collective-permute-done.6), channel_id=1, source_target_pairs={{256,0},{273,1},{290,2},{307,3},{324,4},{341,5},{358,6},{375,7},{3... | collective-permute-start | bytes 1179656 | tf_op jit(solution)/shard_map/ppermute | solution.py:18
  64.0 52.8 %collective-permute-start.2 = (f32[3,128,128]{2,1,0:T(8,128)S(1)}, f32[3,128,128]{2,1,0:T(8,128)S(1)}, u32[]{:S(2)}, u32[]{:S(2)}) collective-permute-start(f32[3,128,128]{2,1,0:T(8,128)S(1)} %collective-permute-done.1.refs_1_), channel_id=1, source_target_pairs={{1,0},{2,1},{3,2},{4,3},{5,4},{6,5},{7,6},{8,7},{9,8},{10,9},{11,1... | collective-permute-start | bytes 589832 | tf_op jit(solution)/shard_map/ppermute | solution.py:18
  75.9 70.5 %collective-permute-start.13 = (f32[6,128,128]{2,1,0:T(8,128)S(1)}, f32[6,128,128]{2,1,0:T(8,128)S(1)}, u32[]{:S(2)}, u32[]{:S(2)}) collective-permute-start(f32[6,128,128]{2,1,0:T(8,128)S(1)} %collective-permute-done.12.refs_4_), channel_id=1, source_target_pairs={{16,0},{17,1},{18,2},{19,3},{20,4},{21,5},{22,6},{23,7},{24,8},{25... | collective-permute-start | bytes 1179656 | tf_op jit(solution)/shard_map/ppermute | solution.py:18
  81.9 73.0 %collective-permute-start.15 = (f32[6,128,128]{2,1,0:T(8,128)S(1)}, f32[6,128,128]{2,1,0:T(8,128)S(1)}, u32[]{:S(2)}, u32[]{:S(2)}) collective-permute-start(f32[6,128,128]{2,1,0:T(8,128)S(1)} %collective-permute-done.14.refs_5_), channel_id=1, source_target_pairs={{16,0},{17,1},{18,2},{19,3},{20,4},{21,5},{22,6},{23,7},{24,8},{25... | collective-permute-start | bytes 1179656 | tf_op jit(solution)/shard_map/ppermute | solution.py:18
  116.8 27.5 %collective-permute-start.4 = (f32[3,128,128]{2,1,0:T(8,128)S(1)}, f32[3,128,128]{2,1,0:T(8,128)S(1)}, u32[]{:S(2)}, u32[]{:S(2)}) collective-permute-start(f32[3,128,128]{2,1,0:T(8,128)S(1)} %collective-permute-done.3.refs_2_), channel_id=1, source_target_pairs={{1,0},{2,1},{3,2},{4,3},{5,4},{6,5},{7,6},{8,7},{9,8},{10,9},{11,1... | collective-permute-start | bytes 589832 | tf_op jit(solution)/shard_map/ppermute | solution.py:18
  137.9 25.4 %collective-permute-start.10 = (f32[6,128,128]{2,1,0:T(8,128)S(1)}, f32[6,128,128]{2,1,0:T(8,128)S(1)}, u32[]{:S(2)}, u32[]{:S(2)}) collective-permute-start(f32[6,128,128]{2,1,0:T(8,128)S(1)} %collective-permute-done.9.refs_5_), channel_id=1, source_target_pairs={{16,0},{17,1},{18,2},{19,3},{20,4},{21,5},{22,6},{23,7},{24,8},{25... | collective-permute-start | bytes 1179656 | tf_op jit(solution)/shard_map/ppermute | solution.py:18
  139.8 31.4 %collective-permute-start.8 = (f32[6,128,128]{2,1,0:T(8,128)S(1)}, f32[6,128,128]{2,1,0:T(8,128)S(1)}, u32[]{:S(2)}, u32[]{:S(2)}) collective-permute-start(f32[6,128,128]{2,1,0:T(8,128)S(1)} %collective-permute-done.7.refs_4_), channel_id=1, source_target_pairs={{16,0},{17,1},{18,2},{19,3},{20,4},{21,5},{22,6},{23,7},{24,8},{25... | collective-permute-start | bytes 1179656 | tf_op jit(solution)/shard_map/ppermute | solution.py:18

commit v2 on v1

--- a/solution.py
+++ b/solution.py
@@ -31,6 +31,8 @@
     flip = scalars[1]
     right_zero = scalars[2]
     first = scalars[3]
+    left_swap = scalars[4]
+    right_swap = scalars[5]
 
     def put_left(slot, block):
         high, low = split(block)
@@ -40,11 +42,11 @@
 
     for pair in range(half):
         pick = jnp.minimum(half - 1 - pair + left_zero, half - 1)
-        block = mirror_a[pick].T
+        block = jnp.where(left_swap == 0, mirror_a[pick], mirror_b[pick]).T
         if pair == 0:
             block = block * (1 - left_zero).astype(jnp.float32)
         put_left(2 * pair, block)
-        put_left(2 * pair + 1, mirror_b[half - 1 - pair].T)
+        put_left(2 * pair + 1, jnp.where(left_swap == 0, mirror_b[half - 1 - pair], mirror_a[half - 1 - pair]).T)
     for slot in range(slots):
         block = stored[slot]
         if slot == 0:
@@ -52,7 +54,7 @@
         put_left(slots + slot, block)
 
     def right_block(layer, slot):
-        swapped = flip if layer == 0 else 1 - flip
+        swapped = (flip + right_swap + layer) % 2
         if mirrored:
             stored_slot = slots - 1 - slot
             swapped = swapped if stored_slot % 2 == 0 else 1 - swapped
@@ -127,69 +129,98 @@
     q = lax.axis_index("col")
     slots = upper.shape[2]
     size = upper.shape[4]
-    b = p % col_count
+    half = slots // 2
+    middle = col_count // 2
 
     def send(value, source_of):
         return permute(value, row_count, col_count, source_of)
 
+    def after(value, *earlier):
+        return lax.optimization_barrier((value, *earlier))[0]
+
+    def shift_of(amount, order):
+        near_is_same = amount < middle
+        return amount if near_is_same == (order == 0) else amount + col_count
+
+    def row_from(p, q):
+        return p - q if (p + q) % 2 == 0 else p + q
+
+    def signed(p, value):
+        return value if p % 2 == 0 else -value
+
+    def from_line(p, line, order):
+        amount = shift_of(line, order)
+        return (p + signed(p, amount), line)
+
+    def sum_source(order):
+        return lambda p, q: from_line(p, signed(p, q) % col_count, order)
+
+    def col_source(order):
+        return lambda p, q: from_line(p, signed(p, q - p) % col_count, order)
+
     present = mask.reshape(slots).astype(jnp.float32)
     stored = upper.reshape(slots, size, size) * present[:, None, None]
-
-    by_parity = stored.reshape(slots // 2, 2, size, size)
+    by_parity = stored.reshape(half, 2, size, size)
     even, odd = by_parity[:, 0], by_parity[:, 1]
-    at_zero = q == 0
-    for_left = jnp.concatenate([jnp.where(at_zero, even, odd), jnp.where(at_zero, odd, even)])
-    via_left = send(for_left, lambda p, q: (p, q - 2 * p))
-    via_upper = send(stored, lambda p, q: (p, p - q))
-    via_lower = send(stored, lambda p, q: (p, q - p))
-    stored_next = send(stored, lambda p, q: (p, q + 1))
-
-    mirror = []
-    upper_right = []
-    lower_right = []
-    for layer in range(2):
-        shift = layer * col_count
-
-        def from_sum(p, q):
-            return (p + q + shift, 2 * p + q)
-
-        half = via_left[layer * (slots // 2) : (layer + 1) * (slots // 2)]
-        mirror.append(send(half, from_sum))
-        upper_right.append(send(via_upper, from_sum))
-    for layer in range(2):
-        shift = layer * col_count
-
-        def from_col(p, q):
-            return (q + p // col_count * col_count + shift, p + q)
-
-        lower_right.append(send(via_lower, from_col))
-
-    def up_one(value):
-        return send(value, lambda p, q: (p + 1, q))
-
-    def along_one(value):
-        return send(value, lambda p, q: (p, q + 1))
-
-    mirror_next = [along_one(value) for value in mirror]
-    upper_next = [up_one(value) for value in upper_right]
-    lower_next = [up_one(value) for value in lower_right]
-
-    def scalars(step, mirrored):
+    target = -q % col_count
+    near_is_other = jnp.where((p + target) % 2 == 0, target >= middle, target > middle)
+    odd_first = (q != 0) != near_is_other
+    for_left = jnp.concatenate([jnp.where(odd_first, odd, even), jnp.where(odd_first, even, odd)])
+
+    via_upper = send(stored, lambda p, q: (p, -row_from(p, q)))
+    via_left = send(for_left, lambda p, q: (p, row_from(p, q) - p))
+    via_lower = send(after(stored, via_upper, via_left), lambda p, q: (p, row_from(p, q) + 1))
+    first = [None, None]
+    second = [None, None]
+    for order in (0, 1):
+        half_of_left = via_left[order * half : (order + 1) * half]
+        first[order] = send(jnp.concatenate([via_upper, half_of_left]), sum_source(order))
+    for order in (0, 1):
+        second[order] = send(via_lower, col_source(order))
+    u_near = send(first[0][:slots], lambda p, q: (p + 1, q))
+    d_near = send(second[0], lambda p, q: (p - 1, q))
+    first[1] = after(first[1], u_near)
+    upper_next = [u_near, send(first[1][:slots], lambda p, q: (p + 1, q))]
+    second[1] = after(second[1], d_near)
+    lower_right = [d_near, send(second[1], lambda p, q: (p - 1, q))]
+    upper_right = [value[:slots] for value in first]
+    mirror = [value[slots:] for value in first]
+    lower_next = second
+    moved = send(jnp.concatenate(mirror), lambda p, q: (p, q + 1))
+    mirror_next = [moved[:half], moved[half:]]
+    stored_next = send(after(stored, first[0], second[0]), lambda p, q: (p, q + 1))
+
+    def scalars(step):
+        row = (p + step) % row_count
         start = (q + step) % col_count
-        right = (-b - step) % col_count
-        target = (q - b) % col_count
-        carry = (start + right - target) // col_count
-        left_zero = (start == 0).astype(jnp.int32)
-        right_zero = (right == 0).astype(jnp.int32)
-        flip = (q + step >= col_count).astype(jnp.int32)
-        first = carry + (right_zero if mirrored else slots)
-        return jnp.stack([left_zero, flip, right_zero, first]).astype(jnp.int32)
+        right = -row % col_count
+        carry = (start + right - (q - p) % col_count) // col_count
+        left_zero = start == 0
+        right_zero = right == 0
+        flip = q + step >= col_count
+        left_swap = jnp.where(p % 2 == 0, start >= middle, start > middle)
+        upper_swap = jnp.where(row % 2 == 0, q >= middle, q > middle)
+        landed = (row - 1) % row_count
+        sign = 1 - 2 * (landed % 2)
+        amount = sign * (q - landed) % col_count
+        near = landed + sign * amount + jnp.where(amount < middle, 0, col_count)
+        lower_swap = ((near - q) % row_count // col_count + row // col_count) % 2
+        return left_zero, flip, right_zero, carry, left_swap, upper_swap, lower_swap
+
+    def packed(*values):
+        return jnp.stack([jnp.asarray(value, jnp.int32) for value in values])
+
+    def right_scalars(step, mirrored):
+        left_zero, flip, right_zero, carry, left_swap, upper_swap, lower_swap = scalars(step)
+        if mirrored:
+            return packed(left_zero, flip, right_zero, carry + right_zero, left_swap, lower_swap)
+        return packed(left_zero, flip, right_zero, carry + slots, left_swap, upper_swap)
 
     total = jnp.zeros((4 * slots, size, size), jnp.float32)
-    total = add_products(total, False, scalars(0, False), *mirror, stored, *upper_right)
-    total = add_products(total, False, scalars(1, False), *mirror_next, stored_next, *upper_next)
-    total = add_products(total, True, scalars(0, True), *mirror, stored, *lower_right)
-    total = add_products(total, True, scalars(1, True), *mirror_next, stored_next, *lower_next)
+    total = add_products(total, False, right_scalars(0, False), *mirror, stored, *upper_right)
+    total = add_products(total, True, right_scalars(1, True), *mirror_next, stored_next, *lower_next)
+    total = add_products(total, False, right_scalars(1, False), *mirror_next, stored_next, *upper_next)
+    total = add_products(total, True, right_scalars(0, True), *mirror, stored, *lower_right)
     return total.reshape(1, 1, 4 * slots, 1, size, size)
 
 

time: 175 us -> 170 us (0.971)
  the two profiles are of different devices: /device:TPU:16 before, /device:TPU:224 now
where the time goes in v2:
time: 170 us; the launch traced here: 169 us
  starting transfers between devices  99.3 us (58%)
  waiting for transfers between devices  54.6 us (32%)
  Pallas kernels  9.8 us (6%)
  other arithmetic  2.88 us (2%)
  local copies, waits for them, and re-layouts  1.83 us (1%)
    ppermute x13, starting transfers between devices, permute(): return lax.ppermute(value, MESH_AXES, pairs)  99.3 us
    ppermute x13, waiting for transfers between devices, permute(): return lax.ppermute(value, MESH_AXES, pairs)  54.6 us
    pallas_call x4, Pallas kernels, add_products(): pl.pallas_call(kernel, out_shape=jax.ShapeDtypeStruct(total.shape, jnp.fl...  9.8 us
  transfers between devices with their start and end apart: 13, of which 5 were waited for; matrix products, arithmetic and copies ran while one was open for 1% of the time, Pallas kernels for 4%

profile of v2, /device:TPU:224, one launch (start us, length us, event | category | flops | bytes accessed | tf_op | source)
XLA Modules:
  0.0 169.2 jit_solution(11877946181896495702)
XLA Ops:
  0.0 0.0 copy-start.2
  0.0 0.0 copy-start
  0.0 0.7 convert_reduce_fusion
  0.7 0.1 convert_element_type.20
  0.8 0.1 copy.5
  0.9 1.1 copy_multiply_fusion
  2.1 0.7 collective-permute-start.1
  2.8 0.0 copy-done.2
  2.8 0.0 copy-done
  2.8 0.1 bitcast_multiply_fusion.refs_3_
  2.9 8.3 %collective-permute-start = (f32[6,128,128]{2,1,0:T(8,128)S(1)}, f32[6,128,128]{2,1,0:T(8,128)S(1)}, u32[]{:S(2)}, u32[]{:S(2)}) collective-permute-start(f32[6,128,128]{2,1,0:T(8,128)S(1)} %bitcast_multiply_fusion.refs_3_), channel_id=1, source_target_pairs={{0,0},{15,1},{2,2},{13,3},{4,4},{11,5},{6,6},{9,7},{8,8},{7,9},{10... | collective-permute-start | bytes 1179656 | tf_op jit(solution)/shard_map/ppermute | solution.py:18
  11.2 0.0 collective-permute-done.1
  11.3 11.4 %collective-permute-done = f32[6,128,128]{2,1,0:T(8,128)S(1)} collective-permute-done((f32[6,128,128]{2,1,0:T(8,128)S(1)}, f32[6,128,128]{2,1,0:T(8,128)S(1)}, u32[]{:S(2)}, u32[]{:S(2)}) %collective-permute-start) | collective-permute-done | bytes 393248 | tf_op jit(solution)/shard_map/ppermute | solution.py:18
  22.6 0.1 pad_maximum_fusion
  22.8 0.7 collective-permute-start.2
  23.5 6.4 %collective-permute-start.5 = (f32[6,128,128]{2,1,0:T(8,128)S(1)}, f32[6,128,128]{2,1,0:T(8,128)}, u32[]{:S(2)}, u32[]{:S(2)}) collective-permute-start(f32[6,128,128]{2,1,0:T(8,128)S(1)} %bitcast_multiply_fusion.refs_3_), channel_id=1, source_target_pairs={{1,0},{2,1},{15,2},{4,3},{13,4},{6,5},{11,6},{8,7},{9,8},{10,9},{7... | collective-permute-start | bytes 1179656 | tf_op jit(solution)/shard_map/ppermute | solution.py:18
  29.9 8.2 %collective-permute-start.3 = (f32[9,128,128]{2,1,0:T(8,128)S(1)}, f32[9,128,128]{2,1,0:T(8,128)S(1)}, u32[]{:S(2)}, u32[]{:S(2)}) collective-permute-start(f32[9,128,128]{2,1,0:T(8,128)S(1)} %get-tuple-element.15), channel_id=1, source_target_pairs={{256,0},{273,1},{290,2},{307,3},{324,4},{341,5},{358,6},{375,7},{1... | collective-permute-start | bytes 1769480 | tf_op jit(solution)/shard_map/ppermute | solution.py:18
  38.1 0.0 collective-permute-done.5
  38.1 3.5 %collective-permute-start.6 = (f32[6,128,128]{2,1,0:T(8,128)}, f32[6,128,128]{2,1,0:T(8,128)S(1)}, u32[]{:S(2)}, u32[]{:S(2)}) collective-permute-start(f32[6,128,128]{2,1,0:T(8,128)} %collective-permute-done.5), channel_id=1, source_target_pairs={{0,0},{17,1},{34,2},{51,3},{68,4},{85,5},{102,6},{119,7},{392,8},{... | collective-permute-start | bytes 1179656 | tf_op jit(solution)/shard_map/ppermute | solution.py:18
  41.6 0.0 collective-permute-done.2
  41.7 8.2 %collective-permute-start.4 = (f32[6,128,128]{2,1,0:T(8,128)S(1)}, f32[6,128,128]{2,1,0:T(8,128)S(1)}, u32[]{:S(2)}, u32[]{:S(2)}) collective-permute-start(f32[6,128,128]{2,1,0:T(8,128)S(1)} %slice.47.refs_4_), channel_id=1, source_target_pairs={{16,0},{17,1},{18,2},{19,3},{20,4},{21,5},{22,6},{23,7},{24,8},{25... | collective-permute-start | bytes 1179656 | tf_op jit(solution)/shard_map/ppermute | solution.py:18
  49.9 32.7 %collective-permute-start.8 = (f32[6,128,128]{2,1,0:T(8,128)}, f32[6,128,128]{2,1,0:T(8,128)S(1)}, u32[]{:S(2)}, u32[]{:S(2)}) collective-permute-start(f32[6,128,128]{2,1,0:T(8,128)} %collective-permute-done.5), channel_id=1, source_target_pairs={{256,0},{273,1},{290,2},{307,3},{324,4},{341,5},{358,6},{375,7},{1... | collective-permute-start | bytes 1179656 | tf_op jit(solution)/shard_map/ppermute | solution.py:18
  82.6 0.0 collective-permute-done.6.refs_4_
  82.6 3.6 %collective-permute-start.7 = (f32[6,128,128]{2,1,0:T(8,128)S(1)}, f32[6,128,128]{2,1,0:T(8,128)S(1)}, u32[]{:S(2)}, u32[]{:S(2)}) collective-permute-start(f32[6,128,128]{2,1,0:T(8,128)S(1)} %collective-permute-done.6.refs_4_), channel_id=1, source_target_pairs={{496,0},{497,1},{498,2},{499,3},{500,4},{501,5},{502,6},{503,7},{5... | collective-permute-start | bytes 1179656 | tf_op jit(solution)/shard_map/ppermute | solution.py:18
  86.2 4.4 %collective-permute-done.3 = f32[9,128,128]{2,1,0:T(8,128)S(1)} collective-permute-done((f32[9,128,128]{2,1,0:T(8,128)S(1)}, f32[9,128,128]{2,1,0:T(8,128)S(1)}, u32[]{:S(2)}, u32[]{:S(2)}) %collective-permute-start.3) | collective-permute-done | bytes 589856 | tf_op jit(solution)/shard_map/ppermute | solution.py:18
  90.6 11.6 %collective-permute-done.4.refs_4_ = f32[6,128,128]{2,1,0:T(8,128)S(1)} collective-permute-done((f32[6,128,128]{2,1,0:T(8,128)S(1)}, f32[6,128,128]{2,1,0:T(8,128)S(1)}, u32[]{:S(2)}, u32[]{:S(2)}) %collective-permute-start.4) | collective-permute-done | bytes 393248 | tf_op jit(solution)/shard_map/ppermute | solution.py:18
  102.3 0.0 copy-done.1
  102.3 0.8 pad_maximum_fusion.3
  103.1 1.9 %collective-permute-start.10 = (f32[6,128,128]{2,1,0:T(8,128)}, f32[6,128,128]{2,1,0:T(8,128)S(1)}, u32[]{:S(2)}, u32[]{:S(2)}) collective-permute-start(f32[6,128,128]{2,1,0:T(8,128)} %pad_maximum_fusion.3), channel_id=1, source_target_pairs={{1,0},{2,1},{3,2},{4,3},{5,4},{6,5},{7,6},{8,7},{9,8},{10,9},{11,1... | collective-permute-start | bytes 1179656 | tf_op jit(solution)/shard_map/ppermute | solution.py:18
  105.0 1.9 %collective-permute-start.11 = (f32[6,128,128]{2,1,0:T(8,128)S(1)}, f32[6,128,128]{2,1,0:T(8,128)S(1)}, u32[]{:S(2)}, u32[]{:S(2)}) collective-permute-start(f32[6,128,128]{2,1,0:T(8,128)S(1)} %bitcast_multiply_fusion.refs_3_), channel_id=1, source_target_pairs={{1,0},{2,1},{3,2},{4,3},{5,4},{6,5},{7,6},{8,7},{9,8},{10,9},{11,1... | collective-permute-start | bytes 1179656 | tf_op jit(solution)/shard_map/ppermute | solution.py:18
  107.4 0.1 stack.115.refs_0_
  107.5 0.1 stack.112.refs_0_
  107.5 0.1 stack.119.refs_0_
  107.6 0.1 stack.101.refs_0_
  107.7 1.0 slice.41.refs_5_
  108.7 7.2 %collective-permute-start.12 = (f32[6,128,128]{2,1,0:T(8,128)S(1)}, f32[6,128,128]{2,1,0:T(8,128)S(1)}, u32[]{:S(2)}, u32[]{:S(2)}) collective-permute-start(f32[6,128,128]{2,1,0:T(8,128)S(1)} %slice.41.refs_5_), channel_id=1, source_target_pairs={{16,0},{17,1},{18,2},{19,3},{20,4},{21,5},{22,6},{23,7},{24,8},{25... | collective-permute-start | bytes 1179656 | tf_op jit(solution)/shard_map/ppermute | solution.py:18
  116.0 0.2 broadcast_in_dim.4.refs_6_
  116.1 2.1 %shard_map.28.refs_6_ = f32[24,128,128]{2,1,0:T(8,128)S(1)} custom-call(s32[6]{0:T(128)S(1)} %stack.119.refs_0_, f32[3,128,128]{2,1,0:T(8,128)S(1)} %slice.45.refs_1_, f32[3,128,128]{2,1,0:T(8,128)S(1)} %slice.38.refs_2_, f32[6,128,128]{2,1,0:T(8,128)S(1)} %bitcast_multiply_fusion.refs_3_, f32[6,128,128]{2,1,0:T(8,128)S(1)} %slice.47.refs_4_, ...), custom_call_target="tpu_custom_call" | custom-call | flops 905969664 | bytes 4194304 | tf_op jit(solution)/shard_map/pallas_call | solution.py:109
  118.3 12.3 %collective-permute-done.8.refs_5_ = f32[6,128,128]{2,1,0:T(8,128)S(1)} collective-permute-done((f32[6,128,128]{2,1,0:T(8,128)}, f32[6,128,128]{2,1,0:T(8,128)S(1)}, u32[]{:S(2)}, u32[]{:S(2)}) %collective-permute-start.8) | collective-permute-done | bytes 393248 | tf_op jit(solution)/shard_map/ppermute | solution.py:18
  130.6 0.0 collective-permute-done.7.refs_4_
  130.6 16.0 %collective-permute-start.9 = (f32[6,128,128]{2,1,0:T(8,128)S(1)}, f32[6,128,128]{2,1,0:T(8,128)S(1)}, u32[]{:S(2)}, u32[]{:S(2)}) collective-permute-start(f32[6,128,128]{2,1,0:T(8,128)S(1)} %collective-permute-done.8.refs_5_), channel_id=1, source_target_pairs={{496,0},{497,1},{498,2},{499,3},{500,4},{501,5},{502,6},{503,7},{5... | collective-permute-start | bytes 1179656 | tf_op jit(solution)/shard_map/ppermute | solution.py:18
  146.6 0.0 collective-permute-done.10
  146.7 0.0 collective-permute-done.11.refs_3_
  146.7 2.2 %shard_map.29.refs_6_ = f32[24,128,128]{2,1,0:T(8,128)S(1)} custom-call(s32[6]{0:T(128)S(1)} %stack.115.refs_0_, f32[3,128,128]{2,1,0:T(8,128)S(1)} %get-tuple-element.14.refs_1_, f32[3,128,128]{2,1,0:T(8,128)S(1)} %get-tuple-element.13.refs_2_, f32[6,128,128]{2,1,0:T(8,128)S(1)} %collective-permute-done.11.refs_3_, ...), custom_call_target="tpu_custom_call" | custom-call | flops 905969664 | bytes 4194304 | tf_op jit(solution)/shard_map/pallas_call | solution.py:109
  148.9 14.8 %collective-permute-done.12.refs_5_ = f32[6,128,128]{2,1,0:T(8,128)S(1)} collective-permute-done((f32[6,128,128]{2,1,0:T(8,128)S(1)}, f32[6,128,128]{2,1,0:T(8,128)S(1)}, u32[]{:S(2)}, u32[]{:S(2)}) %collective-permute-start.12) | collective-permute-done | bytes 393248 | tf_op jit(solution)/shard_map/ppermute | solution.py:18
  163.7 2.1 %shard_map.30.refs_6_ = f32[24,128,128]{2,1,0:T(8,128)S(1)} custom-call(s32[6]{0:T(128)S(1)} %stack.112.refs_0_, f32[3,128,128]{2,1,0:T(8,128)S(1)} %get-tuple-element.14.refs_1_, f32[3,128,128]{2,1,0:T(8,128)S(1)} %get-tuple-element.13.refs_2_, f32[6,128,128]{2,1,0:T(8,128)S(1)} %collective-permute-done.11.refs_3_, ...), custom_call_target="tpu_custom_call" | custom-call | flops 905969664 | bytes 4194304 | tf_op jit(solution)/shard_map/pallas_call | solution.py:109
  165.8 0.0 collective-permute-done.9.refs_5_
  165.8 3.3 %shard_map.31 = f32[24,128,128]{2,1,0:T(8,128)} custom-call(s32[6]{0:T(128)S(1)} %stack.101.refs_0_, f32[3,128,128]{2,1,0:T(8,128)S(1)} %slice.45.refs_1_, f32[3,128,128]{2,1,0:T(8,128)S(1)} %slice.38.refs_2_, f32[6,128,128]{2,1,0:T(8,128)S(1)} %bitcast_multiply_fusion.refs_3_, f32[6,128,128]{2,1,0:T(8,128)S(1)} %collective-permute-done.7.refs_4_, ...), custom_call_target="tpu_custom_call" | custom-call | flops 905969664 | bytes 4194304 | tf_op jit(solution)/shard_map/pallas_call | solution.py:109
  (9 shorter events, 0.2 us)
Async XLA Ops:
  0.0 2.8 %copy-start.2 = (s32[1,1,6,1]{2,3,1,0:T(1,128)S(1)}, s32[1,1,6,1]{2,3,1,0:T(1,128)}, u32[]{:S(2)}) copy-start(s32[1,1,6,1]{2,3,1,0:T(1,128)} %param.3) | copy-start | bytes 76
  0.0 2.8 %copy-start = (f32[1,1,6,1,128,128]{5,4,3,2,1,0:T(8,128)S(1)}, f32[1,1,6,1,128,128]{5,4,3,2,1,0:T(8,128)}, u32[]{:S(2)}) copy-start(f32[1,1,6,1,128,128]{5,4,3,2,1,0:T(8,128)} %param.2) | copy-start | bytes 1179652
  2.1 9.1 %collective-permute-start.1 = (f32[6,128,128]{2,1,0:T(8,128)S(1)}, f32[6,128,128]{2,1,0:T(8,128)S(1)}, u32[]{:S(2)}, u32[]{:S(2)}) collective-permute-start(f32[6,128,128]{2,1,0:T(8,128)S(1)} %pad_maximum_fusion.2), channel_id=1, source_target_pairs={{0,0},{1,1},{14,2},{3,3},{12,4},{5,5},{10,6},{7,7},{8,8},{9,9},{6,... | collective-permute-start | bytes 1179656 | tf_op jit(solution)/shard_map/ppermute | solution.py:18
  2.9 19.7 %collective-permute-start = (f32[6,128,128]{2,1,0:T(8,128)S(1)}, f32[6,128,128]{2,1,0:T(8,128)S(1)}, u32[]{:S(2)}, u32[]{:S(2)}) collective-permute-start(f32[6,128,128]{2,1,0:T(8,128)S(1)} %bitcast_multiply_fusion.refs_3_), channel_id=1, source_target_pairs={{0,0},{15,1},{2,2},{13,3},{4,4},{11,5},{6,6},{9,7},{8,8},{7,9},{10... | collective-permute-start | bytes 1179656 | tf_op jit(solution)/shard_map/ppermute | solution.py:18
  22.8 18.9 %collective-permute-start.2 = (f32[9,128,128]{2,1,0:T(8,128)S(1)}, f32[9,128,128]{2,1,0:T(8,128)S(1)}, u32[]{:S(2)}, u32[]{:S(2)}) collective-permute-start(f32[9,128,128]{2,1,0:T(8,128)S(1)} %get-tuple-element.16), channel_id=1, source_target_pairs={{0,0},{17,1},{34,2},{51,3},{68,4},{85,5},{102,6},{119,7},{392,8},{... | collective-permute-start | bytes 1769480 | tf_op jit(solution)/shard_map/ppermute | solution.py:18
  23.5 14.6 %collective-permute-start.5 = (f32[6,128,128]{2,1,0:T(8,128)S(1)}, f32[6,128,128]{2,1,0:T(8,128)}, u32[]{:S(2)}, u32[]{:S(2)}) collective-permute-start(f32[6,128,128]{2,1,0:T(8,128)S(1)} %bitcast_multiply_fusion.refs_3_), channel_id=1, source_target_pairs={{1,0},{2,1},{15,2},{4,3},{13,4},{6,5},{11,6},{8,7},{9,8},{10,9},{7... | collective-permute-start | bytes 1179656 | tf_op jit(solution)/shard_map/ppermute | solution.py:18
  29.9 60.8 %collective-permute-start.3 = (f32[9,128,128]{2,1,0:T(8,128)S(1)}, f32[9,128,128]{2,1,0:T(8,128)S(1)}, u32[]{:S(2)}, u32[]{:S(2)}) collective-permute-start(f32[9,128,128]{2,1,0:T(8,128)S(1)} %get-tuple-element.15), channel_id=1, source_target_pairs={{256,0},{273,1},{290,2},{307,3},{324,4},{341,5},{358,6},{375,7},{1... | collective-permute-start | bytes 1769480 | tf_op jit(solution)/shard_map/ppermute | solution.py:18
  38.1 44.5 %collective-permute-start.6 = (f32[6,128,128]{2,1,0:T(8,128)}, f32[6,128,128]{2,1,0:T(8,128)S(1)}, u32[]{:S(2)}, u32[]{:S(2)}) collective-permute-start(f32[6,128,128]{2,1,0:T(8,128)} %collective-permute-done.5), channel_id=1, source_target_pairs={{0,0},{17,1},{34,2},{51,3},{68,4},{85,5},{102,6},{119,7},{392,8},{... | collective-permute-start | bytes 1179656 | tf_op jit(solution)/shard_map/ppermute | solution.py:18
  41.7 60.6 %collective-permute-start.4 = (f32[6,128,128]{2,1,0:T(8,128)S(1)}, f32[6,128,128]{2,1,0:T(8,128)S(1)}, u32[]{:S(2)}, u32[]{:S(2)}) collective-permute-start(f32[6,128,128]{2,1,0:T(8,128)S(1)} %slice.47.refs_4_), channel_id=1, source_target_pairs={{16,0},{17,1},{18,2},{19,3},{20,4},{21,5},{22,6},{23,7},{24,8},{25... | collective-permute-start | bytes 1179656 | tf_op jit(solution)/shard_map/ppermute | solution.py:18
  49.9 80.7 %collective-permute-start.8 = (f32[6,128,128]{2,1,0:T(8,128)}, f32[6,128,128]{2,1,0:T(8,128)S(1)}, u32[]{:S(2)}, u32[]{:S(2)}) collective-permute-start(f32[6,128,128]{2,1,0:T(8,128)} %collective-permute-done.5), channel_id=1, source_target_pairs={{256,0},{273,1},{290,2},{307,3},{324,4},{341,5},{358,6},{375,7},{1... | collective-permute-start | bytes 1179656 | tf_op jit(solution)/shard_map/ppermute | solution.py:18
  82.6 48.0 %collective-permute-start.7 = (f32[6,128,128]{2,1,0:T(8,128)S(1)}, f32[6,128,128]{2,1,0:T(8,128)S(1)}, u32[]{:S(2)}, u32[]{:S(2)}) collective-permute-start(f32[6,128,128]{2,1,0:T(8,128)S(1)} %collective-permute-done.6.refs_4_), channel_id=1, source_target_pairs={{496,0},{497,1},{498,2},{499,3},{500,4},{501,5},{502,6},{503,7},{5... | collective-permute-start | bytes 1179656 | tf_op jit(solution)/shard_map/ppermute | solution.py:18
  90.6 11.6 %copy-start.1 = (f32[9,128,128]{2,1,0:T(8,128)}, f32[9,128,128]{2,1,0:T(8,128)S(1)}, u32[]{:S(2)}) copy-start(f32[9,128,128]{2,1,0:T(8,128)S(1)} %collective-permute-done.3) | copy-start | bytes 1769476
  103.1 43.6 %collective-permute-start.10 = (f32[6,128,128]{2,1,0:T(8,128)}, f32[6,128,128]{2,1,0:T(8,128)S(1)}, u32[]{:S(2)}, u32[]{:S(2)}) collective-permute-start(f32[6,128,128]{2,1,0:T(8,128)} %pad_maximum_fusion.3), channel_id=1, source_target_pairs={{1,0},{2,1},{3,2},{4,3},{5,4},{6,5},{7,6},{8,7},{9,8},{10,9},{11,1... | collective-permute-start | bytes 1179656 | tf_op jit(solution)/shard_map/ppermute | solution.py:18
  105.0 41.7 %collective-permute-start.11 = (f32[6,128,128]{2,1,0:T(8,128)S(1)}, f32[6,128,128]{2,1,0:T(8,128)S(1)}, u32[]{:S(2)}, u32[]{:S(2)}) collective-permute-start(f32[6,128,128]{2,1,0:T(8,128)S(1)} %bitcast_multiply_fusion.refs_3_), channel_id=1, source_target_pairs={{1,0},{2,1},{3,2},{4,3},{5,4},{6,5},{7,6},{8,7},{9,8},{10,9},{11,1... | collective-permute-start | bytes 1179656 | tf_op jit(solution)/shard_map/ppermute | solution.py:18
  108.7 54.9 %collective-permute-start.12 = (f32[6,128,128]{2,1,0:T(8,128)S(1)}, f32[6,128,128]{2,1,0:T(8,128)S(1)}, u32[]{:S(2)}, u32[]{:S(2)}) collective-permute-start(f32[6,128,128]{2,1,0:T(8,128)S(1)} %slice.41.refs_5_), channel_id=1, source_target_pairs={{16,0},{17,1},{18,2},{19,3},{20,4},{21,5},{22,6},{23,7},{24,8},{25... | collective-permute-start | bytes 1179656 | tf_op jit(solution)/shard_map/ppermute | solution.py:18
  130.6 35.2 %collective-permute-start.9 = (f32[6,128,128]{2,1,0:T(8,128)S(1)}, f32[6,128,128]{2,1,0:T(8,128)S(1)}, u32[]{:S(2)}, u32[]{:S(2)}) collective-permute-start(f32[6,128,128]{2,1,0:T(8,128)S(1)} %collective-permute-done.8.refs_5_), channel_id=1, source_target_pairs={{496,0},{497,1},{498,2},{499,3},{500,4},{501,5},{502,6},{503,7},{5... | collective-permute-start | bytes 1179656 | tf_op jit(solution)/shard_map/ppermute | solution.py:18

commit v3 on v2

--- a/solution.py
+++ b/solution.py
@@ -177,12 +177,14 @@
         first[order] = send(jnp.concatenate([via_upper, half_of_left]), sum_source(order))
     for order in (0, 1):
         second[order] = send(via_lower, col_source(order))
-    u_near = send(first[0][:slots], lambda p, q: (p + 1, q))
-    d_near = send(second[0], lambda p, q: (p - 1, q))
-    first[1] = after(first[1], u_near)
-    upper_next = [u_near, send(first[1][:slots], lambda p, q: (p + 1, q))]
-    second[1] = after(second[1], d_near)
-    lower_right = [d_near, send(second[1], lambda p, q: (p - 1, q))]
+    upper_next = [None, None]
+    lower_right = [None, None]
+    upper_next[1] = send(first[1][:slots], lambda p, q: (p + 1, q))
+    lower_right[0] = send(second[0], lambda p, q: (p - 1, q))
+    first[0] = after(first[0], upper_next[1])
+    upper_next[0] = send(first[0][:slots], lambda p, q: (p + 1, q))
+    second[1] = after(second[1], lower_right[0])
+    lower_right[1] = send(second[1], lambda p, q: (p - 1, q))
     upper_right = [value[:slots] for value in first]
     mirror = [value[slots:] for value in first]
     lower_next = second

time: 170 us -> 167 us (0.982)
  the two profiles are of different devices: /device:TPU:224 before, /device:TPU:9 now
where the time goes in v3:
time: 167 us; the launch traced here: 166 us
  waiting for transfers between devices  78.2 us (47%)
  starting transfers between devices  72.2 us (43%)
  Pallas kernels  9.8 us (6%)
  other arithmetic  2.88 us (2%)
  local copies, waits for them, and re-layouts  2.62 us (2%)
    ppermute x13, waiting for transfers between devices, permute(): return lax.ppermute(value, MESH_AXES, pairs)  78.2 us
    ppermute x13, starting transfers between devices, permute(): return lax.ppermute(value, MESH_AXES, pairs)  72.2 us
    pallas_call x4, Pallas kernels, add_products(): pl.pallas_call(kernel, out_shape=jax.ShapeDtypeStruct(total.shape, jnp.fl...  9.8 us
  transfers between devices with their start and end apart: 13, of which 6 were waited for; matrix products, arithmetic and copies ran while one was open for 2% of the time, Pallas kernels for 4%

profile of v3, /device:TPU:9, one launch (start us, length us, event | category | flops | bytes accessed | tf_op | source)
XLA Modules:
  0.0 166.5 jit_solution(9639690364158843679)
XLA Ops:
  0.0 0.0 copy-start.2
  0.0 0.7 convert_reduce_fusion
  0.7 0.1 convert_element_type.20
  0.8 0.1 copy.5
  0.9 1.1 copy_multiply_fusion
  2.1 0.7 collective-permute-start.1
  2.8 0.0 copy-done.2
  2.8 0.0 copy-done
  2.8 0.1 bitcast_multiply_fusion.refs_3_
  2.9 4.1 %collective-permute-start = (f32[6,128,128]{2,1,0:T(8,128)S(1)}, f32[6,128,128]{2,1,0:T(8,128)S(1)}, u32[]{:S(2)}, u32[]{:S(2)}) collective-permute-start(f32[6,128,128]{2,1,0:T(8,128)S(1)} %bitcast_multiply_fusion.refs_3_), channel_id=1, source_target_pairs={{0,0},{15,1},{2,2},{13,3},{4,4},{11,5},{6,6},{9,7},{8,8},{7,9},{10... | collective-permute-start | bytes 1179656 | tf_op jit(solution)/shard_map/ppermute | solution.py:18
  7.1 0.0 collective-permute-done.1
  7.1 9.4 %collective-permute-done = f32[6,128,128]{2,1,0:T(8,128)S(1)} collective-permute-done((f32[6,128,128]{2,1,0:T(8,128)S(1)}, f32[6,128,128]{2,1,0:T(8,128)S(1)}, u32[]{:S(2)}, u32[]{:S(2)}) %collective-permute-start) | collective-permute-done | bytes 393248 | tf_op jit(solution)/shard_map/ppermute | solution.py:18
  16.5 0.1 pad_maximum_fusion
  16.6 21.6 %collective-permute-start.3 = (f32[9,128,128]{2,1,0:T(8,128)S(1)}, f32[9,128,128]{2,1,0:T(8,128)S(1)}, u32[]{:S(2)}, u32[]{:S(2)}) collective-permute-start(f32[9,128,128]{2,1,0:T(8,128)S(1)} %get-tuple-element.15), channel_id=1, source_target_pairs={{256,0},{273,1},{290,2},{307,3},{324,4},{341,5},{358,6},{375,7},{1... | collective-permute-start | bytes 1769480 | tf_op jit(solution)/shard_map/ppermute | solution.py:18
  38.3 1.9 %collective-permute-start.5 = (f32[6,128,128]{2,1,0:T(8,128)S(1)}, f32[6,128,128]{2,1,0:T(8,128)}, u32[]{:S(2)}, u32[]{:S(2)}) collective-permute-start(f32[6,128,128]{2,1,0:T(8,128)S(1)} %bitcast_multiply_fusion.refs_3_), channel_id=1, source_target_pairs={{1,0},{2,1},{15,2},{4,3},{13,4},{6,5},{11,6},{8,7},{9,8},{10,9},{7... | collective-permute-start | bytes 1179656 | tf_op jit(solution)/shard_map/ppermute | solution.py:18
  40.2 1.9 %collective-permute-start.2 = (f32[9,128,128]{2,1,0:T(8,128)S(1)}, f32[9,128,128]{2,1,0:T(8,128)S(1)}, u32[]{:S(2)}, u32[]{:S(2)}) collective-permute-start(f32[9,128,128]{2,1,0:T(8,128)S(1)} %get-tuple-element.16), channel_id=1, source_target_pairs={{0,0},{17,1},{34,2},{51,3},{68,4},{85,5},{102,6},{119,7},{392,8},{... | collective-permute-start | bytes 1769480 | tf_op jit(solution)/shard_map/ppermute | solution.py:18
  42.1 9.6 %collective-permute-done.5 = f32[6,128,128]{2,1,0:T(8,128)} collective-permute-done((f32[6,128,128]{2,1,0:T(8,128)S(1)}, f32[6,128,128]{2,1,0:T(8,128)}, u32[]{:S(2)}, u32[]{:S(2)}) %collective-permute-start.5) | collective-permute-done | bytes 393248 | tf_op jit(solution)/shard_map/ppermute | solution.py:18
  51.7 2.3 %collective-permute-start.6 = (f32[6,128,128]{2,1,0:T(8,128)}, f32[6,128,128]{2,1,0:T(8,128)S(1)}, u32[]{:S(2)}, u32[]{:S(2)}) collective-permute-start(f32[6,128,128]{2,1,0:T(8,128)} %collective-permute-done.5), channel_id=1, source_target_pairs={{0,0},{17,1},{34,2},{51,3},{68,4},{85,5},{102,6},{119,7},{392,8},{... | collective-permute-start | bytes 1179656 | tf_op jit(solution)/shard_map/ppermute | solution.py:18
  54.1 31.7 %collective-permute-done.3 = f32[9,128,128]{2,1,0:T(8,128)S(1)} collective-permute-done((f32[9,128,128]{2,1,0:T(8,128)S(1)}, f32[9,128,128]{2,1,0:T(8,128)S(1)}, u32[]{:S(2)}, u32[]{:S(2)}) %collective-permute-start.3) | collective-permute-done | bytes 589856 | tf_op jit(solution)/shard_map/ppermute | solution.py:18
  85.7 12.8 %collective-permute-start.4 = (f32[6,128,128]{2,1,0:T(8,128)S(1)}, f32[6,128,128]{2,1,0:T(8,128)S(1)}, u32[]{:S(2)}, u32[]{:S(2)}) collective-permute-start(f32[6,128,128]{2,1,0:T(8,128)S(1)} %slice.46.refs_5_), channel_id=1, source_target_pairs={{16,0},{17,1},{18,2},{19,3},{20,4},{21,5},{22,6},{23,7},{24,8},{25... | collective-permute-start | bytes 1179656 | tf_op jit(solution)/shard_map/ppermute | solution.py:18
  98.6 6.3 %collective-permute-start.8 = (f32[6,128,128]{2,1,0:T(8,128)}, f32[6,128,128]{2,1,0:T(8,128)S(1)}, u32[]{:S(2)}, u32[]{:S(2)}) collective-permute-start(f32[6,128,128]{2,1,0:T(8,128)} %collective-permute-done.5), channel_id=1, source_target_pairs={{256,0},{273,1},{290,2},{307,3},{324,4},{341,5},{358,6},{375,7},{1... | collective-permute-start | bytes 1179656 | tf_op jit(solution)/shard_map/ppermute | solution.py:18
  104.9 16.0 %collective-permute-done.6.refs_4_ = f32[6,128,128]{2,1,0:T(8,128)S(1)} collective-permute-done((f32[6,128,128]{2,1,0:T(8,128)}, f32[6,128,128]{2,1,0:T(8,128)S(1)}, u32[]{:S(2)}, u32[]{:S(2)}) %collective-permute-start.6) | collective-permute-done | bytes 393248 | tf_op jit(solution)/shard_map/ppermute | solution.py:18
  120.9 3.1 %collective-permute-start.7 = (f32[6,128,128]{2,1,0:T(8,128)S(1)}, f32[6,128,128]{2,1,0:T(8,128)S(1)}, u32[]{:S(2)}, u32[]{:S(2)}) collective-permute-start(f32[6,128,128]{2,1,0:T(8,128)S(1)} %collective-permute-done.6.refs_4_), channel_id=1, source_target_pairs={{496,0},{497,1},{498,2},{499,3},{500,4},{501,5},{502,6},{503,7},{5... | collective-permute-start | bytes 1179656 | tf_op jit(solution)/shard_map/ppermute | solution.py:18
  124.0 0.0 collective-permute-done.2
  124.0 0.0 copy-start.1
  124.0 0.0 collective-permute-done.4.refs_5_
  124.1 0.8 copy-done.1
  124.9 0.8 pad_maximum_fusion.3
  125.6 1.9 %collective-permute-start.10 = (f32[6,128,128]{2,1,0:T(8,128)}, f32[6,128,128]{2,1,0:T(8,128)S(1)}, u32[]{:S(2)}, u32[]{:S(2)}) collective-permute-start(f32[6,128,128]{2,1,0:T(8,128)} %pad_maximum_fusion.3), channel_id=1, source_target_pairs={{1,0},{2,1},{3,2},{4,3},{5,4},{6,5},{7,6},{8,7},{9,8},{10,9},{11,1... | collective-permute-start | bytes 1179656 | tf_op jit(solution)/shard_map/ppermute | solution.py:18
  127.6 1.9 %collective-permute-start.11 = (f32[6,128,128]{2,1,0:T(8,128)S(1)}, f32[6,128,128]{2,1,0:T(8,128)S(1)}, u32[]{:S(2)}, u32[]{:S(2)}) collective-permute-start(f32[6,128,128]{2,1,0:T(8,128)S(1)} %bitcast_multiply_fusion.refs_3_), channel_id=1, source_target_pairs={{1,0},{2,1},{3,2},{4,3},{5,4},{6,5},{7,6},{8,7},{9,8},{10,9},{11,1... | collective-permute-start | bytes 1179656 | tf_op jit(solution)/shard_map/ppermute | solution.py:18
  130.0 0.1 stack.115.refs_0_
  130.1 0.1 stack.112.refs_0_
  130.1 0.1 stack.119.refs_0_
  130.2 0.1 stack.101.refs_0_
  130.3 1.0 slice.41.refs_4_
  131.3 5.8 %collective-permute-start.12 = (f32[6,128,128]{2,1,0:T(8,128)S(1)}, f32[6,128,128]{2,1,0:T(8,128)S(1)}, u32[]{:S(2)}, u32[]{:S(2)}) collective-permute-start(f32[6,128,128]{2,1,0:T(8,128)S(1)} %slice.41.refs_4_), channel_id=1, source_target_pairs={{16,0},{17,1},{18,2},{19,3},{20,4},{21,5},{22,6},{23,7},{24,8},{25... | collective-permute-start | bytes 1179656 | tf_op jit(solution)/shard_map/ppermute | solution.py:18
  137.2 0.2 broadcast_in_dim.4.refs_6_
  137.3 2.1 %shard_map.28.refs_6_ = f32[24,128,128]{2,1,0:T(8,128)S(1)} custom-call(s32[6]{0:T(128)S(1)} %stack.119.refs_0_, f32[3,128,128]{2,1,0:T(8,128)S(1)} %slice.37.refs_1_, f32[3,128,128]{2,1,0:T(8,128)S(1)} %slice.47.refs_2_, f32[6,128,128]{2,1,0:T(8,128)S(1)} %bitcast_multiply_fusion.refs_3_, f32[6,128,128]{2,1,0:T(8,128)S(1)} %slice.41.refs_4_, ...), custom_call_target="tpu_custom_call" | custom-call | flops 905969664 | bytes 4194304 | tf_op jit(solution)/shard_map/pallas_call | solution.py:109
  139.5 0.0 collective-permute-done.8.refs_5_
  139.5 0.2 collective-permute-done.7.refs_4_
  139.6 7.7 %collective-permute-start.9 = (f32[6,128,128]{2,1,0:T(8,128)S(1)}, f32[6,128,128]{2,1,0:T(8,128)S(1)}, u32[]{:S(2)}, u32[]{:S(2)}) collective-permute-start(f32[6,128,128]{2,1,0:T(8,128)S(1)} %collective-permute-done.8.refs_5_), channel_id=1, source_target_pairs={{496,0},{497,1},{498,2},{499,3},{500,4},{501,5},{502,6},{503,7},{5... | collective-permute-start | bytes 1179656 | tf_op jit(solution)/shard_map/ppermute | solution.py:18
  147.4 0.0 collective-permute-done.10
  147.4 0.0 collective-permute-done.11.refs_3_
  147.4 2.2 %shard_map.29.refs_6_ = f32[24,128,128]{2,1,0:T(8,128)S(1)} custom-call(s32[6]{0:T(128)S(1)} %stack.115.refs_0_, f32[3,128,128]{2,1,0:T(8,128)S(1)} %get-tuple-element.14.refs_1_, f32[3,128,128]{2,1,0:T(8,128)S(1)} %get-tuple-element.13.refs_2_, f32[6,128,128]{2,1,0:T(8,128)S(1)} %collective-permute-done.11.refs_3_, ...), custom_call_target="tpu_custom_call" | custom-call | flops 905969664 | bytes 4194304 | tf_op jit(solution)/shard_map/pallas_call | solution.py:109
  149.6 11.4 %collective-permute-done.12.refs_4_ = f32[6,128,128]{2,1,0:T(8,128)S(1)} collective-permute-done((f32[6,128,128]{2,1,0:T(8,128)S(1)}, f32[6,128,128]{2,1,0:T(8,128)S(1)}, u32[]{:S(2)}, u32[]{:S(2)}) %collective-permute-start.12) | collective-permute-done | bytes 393248 | tf_op jit(solution)/shard_map/ppermute | solution.py:18
  161.0 2.1 %shard_map.30.refs_6_ = f32[24,128,128]{2,1,0:T(8,128)S(1)} custom-call(s32[6]{0:T(128)S(1)} %stack.112.refs_0_, f32[3,128,128]{2,1,0:T(8,128)S(1)} %get-tuple-element.14.refs_1_, f32[3,128,128]{2,1,0:T(8,128)S(1)} %get-tuple-element.13.refs_2_, f32[6,128,128]{2,1,0:T(8,128)S(1)} %collective-permute-done.11.refs_3_, ...), custom_call_target="tpu_custom_call" | custom-call | flops 905969664 | bytes 4194304 | tf_op jit(solution)/shard_map/pallas_call | solution.py:109
  163.1 0.0 collective-permute-done.9.refs_5_
  163.1 3.3 %shard_map.31 = f32[24,128,128]{2,1,0:T(8,128)} custom-call(s32[6]{0:T(128)S(1)} %stack.101.refs_0_, f32[3,128,128]{2,1,0:T(8,128)S(1)} %slice.37.refs_1_, f32[3,128,128]{2,1,0:T(8,128)S(1)} %slice.47.refs_2_, f32[6,128,128]{2,1,0:T(8,128)S(1)} %bitcast_multiply_fusion.refs_3_, f32[6,128,128]{2,1,0:T(8,128)S(1)} %collective-permute-done.7.refs_4_, ...), custom_call_target="tpu_custom_call" | custom-call | flops 905969664 | bytes 4194304 | tf_op jit(solution)/shard_map/pallas_call | solution.py:109
  (9 shorter events, 0.2 us)
Async XLA Ops:
  0.0 2.8 %copy-start.2 = (s32[1,1,6,1]{2,3,1,0:T(1,128)S(1)}, s32[1,1,6,1]{2,3,1,0:T(1,128)}, u32[]{:S(2)}) copy-start(s32[1,1,6,1]{2,3,1,0:T(1,128)} %param.3) | copy-start | bytes 76
  0.0 2.8 %copy-start = (f32[1,1,6,1,128,128]{5,4,3,2,1,0:T(8,128)S(1)}, f32[1,1,6,1,128,128]{5,4,3,2,1,0:T(8,128)}, u32[]{:S(2)}) copy-start(f32[1,1,6,1,128,128]{5,4,3,2,1,0:T(8,128)} %param.2) | copy-start | bytes 1179652
  2.1 5.0 %collective-permute-start.1 = (f32[6,128,128]{2,1,0:T(8,128)S(1)}, f32[6,128,128]{2,1,0:T(8,128)S(1)}, u32[]{:S(2)}, u32[]{:S(2)}) collective-permute-start(f32[6,128,128]{2,1,0:T(8,128)S(1)} %pad_maximum_fusion.2), channel_id=1, source_target_pairs={{0,0},{1,1},{14,2},{3,3},{12,4},{5,5},{10,6},{7,7},{8,8},{9,9},{6,... | collective-permute-start | bytes 1179656 | tf_op jit(solution)/shard_map/ppermute | solution.py:18
  2.9 13.6 %collective-permute-start = (f32[6,128,128]{2,1,0:T(8,128)S(1)}, f32[6,128,128]{2,1,0:T(8,128)S(1)}, u32[]{:S(2)}, u32[]{:S(2)}) collective-permute-start(f32[6,128,128]{2,1,0:T(8,128)S(1)} %bitcast_multiply_fusion.refs_3_), channel_id=1, source_target_pairs={{0,0},{15,1},{2,2},{13,3},{4,4},{11,5},{6,6},{9,7},{8,8},{7,9},{10... | collective-permute-start | bytes 1179656 | tf_op jit(solution)/shard_map/ppermute | solution.py:18
  16.6 69.1 %collective-permute-start.3 = (f32[9,128,128]{2,1,0:T(8,128)S(1)}, f32[9,128,128]{2,1,0:T(8,128)S(1)}, u32[]{:S(2)}, u32[]{:S(2)}) collective-permute-start(f32[9,128,128]{2,1,0:T(8,128)S(1)} %get-tuple-element.15), channel_id=1, source_target_pairs={{256,0},{273,1},{290,2},{307,3},{324,4},{341,5},{358,6},{375,7},{1... | collective-permute-start | bytes 1769480 | tf_op jit(solution)/shard_map/ppermute | solution.py:18
  38.3 13.5 %collective-permute-start.5 = (f32[6,128,128]{2,1,0:T(8,128)S(1)}, f32[6,128,128]{2,1,0:T(8,128)}, u32[]{:S(2)}, u32[]{:S(2)}) collective-permute-start(f32[6,128,128]{2,1,0:T(8,128)S(1)} %bitcast_multiply_fusion.refs_3_), channel_id=1, source_target_pairs={{1,0},{2,1},{15,2},{4,3},{13,4},{6,5},{11,6},{8,7},{9,8},{10,9},{7... | collective-permute-start | bytes 1179656 | tf_op jit(solution)/shard_map/ppermute | solution.py:18
  40.2 83.8 %collective-permute-start.2 = (f32[9,128,128]{2,1,0:T(8,128)S(1)}, f32[9,128,128]{2,1,0:T(8,128)S(1)}, u32[]{:S(2)}, u32[]{:S(2)}) collective-permute-start(f32[9,128,128]{2,1,0:T(8,128)S(1)} %get-tuple-element.16), channel_id=1, source_target_pairs={{0,0},{17,1},{34,2},{51,3},{68,4},{85,5},{102,6},{119,7},{392,8},{... | collective-permute-start | bytes 1769480 | tf_op jit(solution)/shard_map/ppermute | solution.py:18
  51.7 69.2 %collective-permute-start.6 = (f32[6,128,128]{2,1,0:T(8,128)}, f32[6,128,128]{2,1,0:T(8,128)S(1)}, u32[]{:S(2)}, u32[]{:S(2)}) collective-permute-start(f32[6,128,128]{2,1,0:T(8,128)} %collective-permute-done.5), channel_id=1, source_target_pairs={{0,0},{17,1},{34,2},{51,3},{68,4},{85,5},{102,6},{119,7},{392,8},{... | collective-permute-start | bytes 1179656 | tf_op jit(solution)/shard_map/ppermute | solution.py:18
  85.7 38.3 %collective-permute-start.4 = (f32[6,128,128]{2,1,0:T(8,128)S(1)}, f32[6,128,128]{2,1,0:T(8,128)S(1)}, u32[]{:S(2)}, u32[]{:S(2)}) collective-permute-start(f32[6,128,128]{2,1,0:T(8,128)S(1)} %slice.46.refs_5_), channel_id=1, source_target_pairs={{16,0},{17,1},{18,2},{19,3},{20,4},{21,5},{22,6},{23,7},{24,8},{25... | collective-permute-start | bytes 1179656 | tf_op jit(solution)/shard_map/ppermute | solution.py:18
  98.6 40.9 %collective-permute-start.8 = (f32[6,128,128]{2,1,0:T(8,128)}, f32[6,128,128]{2,1,0:T(8,128)S(1)}, u32[]{:S(2)}, u32[]{:S(2)}) collective-permute-start(f32[6,128,128]{2,1,0:T(8,128)} %collective-permute-done.5), channel_id=1, source_target_pairs={{256,0},{273,1},{290,2},{307,3},{324,4},{341,5},{358,6},{375,7},{1... | collective-permute-start | bytes 1179656 | tf_op jit(solution)/shard_map/ppermute | solution.py:18
  120.9 18.7 %collective-permute-start.7 = (f32[6,128,128]{2,1,0:T(8,128)S(1)}, f32[6,128,128]{2,1,0:T(8,128)S(1)}, u32[]{:S(2)}, u32[]{:S(2)}) collective-permute-start(f32[6,128,128]{2,1,0:T(8,128)S(1)} %collective-permute-done.6.refs_4_), channel_id=1, source_target_pairs={{496,0},{497,1},{498,2},{499,3},{500,4},{501,5},{502,6},{503,7},{5... | collective-permute-start | bytes 1179656 | tf_op jit(solution)/shard_map/ppermute | solution.py:18
  124.0 0.8 copy-start.1
  125.6 21.7 %collective-permute-start.10 = (f32[6,128,128]{2,1,0:T(8,128)}, f32[6,128,128]{2,1,0:T(8,128)S(1)}, u32[]{:S(2)}, u32[]{:S(2)}) collective-permute-start(f32[6,128,128]{2,1,0:T(8,128)} %pad_maximum_fusion.3), channel_id=1, source_target_pairs={{1,0},{2,1},{3,2},{4,3},{5,4},{6,5},{7,6},{8,7},{9,8},{10,9},{11,1... | collective-permute-start | bytes 1179656 | tf_op jit(solution)/shard_map/ppermute | solution.py:18
  127.6 19.9 %collective-permute-start.11 = (f32[6,128,128]{2,1,0:T(8,128)S(1)}, f32[6,128,128]{2,1,0:T(8,128)S(1)}, u32[]{:S(2)}, u32[]{:S(2)}) collective-permute-start(f32[6,128,128]{2,1,0:T(8,128)S(1)} %bitcast_multiply_fusion.refs_3_), channel_id=1, source_target_pairs={{1,0},{2,1},{3,2},{4,3},{5,4},{6,5},{7,6},{8,7},{9,8},{10,9},{11,1... | collective-permute-start | bytes 1179656 | tf_op jit(solution)/shard_map/ppermute | solution.py:18
  131.3 29.7 %collective-permute-start.12 = (f32[6,128,128]{2,1,0:T(8,128)S(1)}, f32[6,128,128]{2,1,0:T(8,128)S(1)}, u32[]{:S(2)}, u32[]{:S(2)}) collective-permute-start(f32[6,128,128]{2,1,0:T(8,128)S(1)} %slice.41.refs_4_), channel_id=1, source_target_pairs={{16,0},{17,1},{18,2},{19,3},{20,4},{21,5},{22,6},{23,7},{24,8},{25... | collective-permute-start | bytes 1179656 | tf_op jit(solution)/shard_map/ppermute | solution.py:18
  139.6 23.5 %collective-permute-start.9 = (f32[6,128,128]{2,1,0:T(8,128)S(1)}, f32[6,128,128]{2,1,0:T(8,128)S(1)}, u32[]{:S(2)}, u32[]{:S(2)}) collective-permute-start(f32[6,128,128]{2,1,0:T(8,128)S(1)} %collective-permute-done.8.refs_5_), channel_id=1, source_target_pairs={{496,0},{497,1},{498,2},{499,3},{500,4},{501,5},{502,6},{503,7},{5... | collective-permute-start | bytes 1179656 | tf_op jit(solution)/shard_map/ppermute | solution.py:18

commit v4 on v3

--- a/solution.py
+++ b/solution.py
@@ -169,7 +169,7 @@
 
     via_upper = send(stored, lambda p, q: (p, -row_from(p, q)))
     via_left = send(for_left, lambda p, q: (p, row_from(p, q) - p))
-    via_lower = send(after(stored, via_upper, via_left), lambda p, q: (p, row_from(p, q) + 1))
+    via_lower = send(after(stored, via_left), lambda p, q: (p, row_from(p, q) + 1))
     first = [None, None]
     second = [None, None]
     for order in (0, 1):

time: 167 us -> 167 us (level)
  no operation moved by 1% of the time
where the time goes in v4:
time: 167 us; the launch traced here: 166 us
  waiting for transfers between devices  78.2 us (47%)
  starting transfers between devices  72.2 us (43%)
  Pallas kernels  9.8 us (6%)
  other arithmetic  2.88 us (2%)
  local copies, waits for them, and re-layouts  2.62 us (2%)
    ppermute x13, waiting for transfers between devices, permute(): return lax.ppermute(value, MESH_AXES, pairs)  78.2 us
    ppermute x13, starting transfers between devices, permute(): return lax.ppermute(value, MESH_AXES, pairs)  72.2 us
    pallas_call x4, Pallas kernels, add_products(): pl.pallas_call(kernel, out_shape=jax.ShapeDtypeStruct(total.shape, jnp.fl...  9.8 us
  transfers between devices with their start and end apart: 13, of which 6 were waited for; matrix products, arithmetic and copies ran while one was open for 2% of the time, Pallas kernels for 4%

profile of v4, /device:TPU:9, one launch (start us, length us, event | category | flops | bytes accessed | tf_op | source)
XLA Modules:
  0.0 166.5 jit_solution(9639690364158843679)
XLA Ops:
  0.0 0.0 copy-start.2
  0.0 0.7 convert_reduce_fusion
  0.7 0.1 convert_element_type.20
  0.8 0.1 copy.5
  0.9 1.1 copy_multiply_fusion
  2.1 0.7 collective-permute-start.1
  2.8 0.0 copy-done.2
  2.8 0.0 copy-done
  2.8 0.1 bitcast_multiply_fusion.refs_3_
  2.9 4.1 %collective-permute-start = (f32[6,128,128]{2,1,0:T(8,128)S(1)}, f32[6,128,128]{2,1,0:T(8,128)S(1)}, u32[]{:S(2)}, u32[]{:S(2)}) collective-permute-start(f32[6,128,128]{2,1,0:T(8,128)S(1)} %bitcast_multiply_fusion.refs_3_), channel_id=1, source_target_pairs={{0,0},{15,1},{2,2},{13,3},{4,4},{11,5},{6,6},{9,7},{8,8},{7,9},{10... | collective-permute-start | bytes 1179656 | tf_op jit(solution)/shard_map/ppermute | solution.py:18
  7.1 0.0 collective-permute-done.1
  7.1 9.4 %collective-permute-done = f32[6,128,128]{2,1,0:T(8,128)S(1)} collective-permute-done((f32[6,128,128]{2,1,0:T(8,128)S(1)}, f32[6,128,128]{2,1,0:T(8,128)S(1)}, u32[]{:S(2)}, u32[]{:S(2)}) %collective-permute-start) | collective-permute-done | bytes 393248 | tf_op jit(solution)/shard_map/ppermute | solution.py:18
  16.5 0.1 pad_maximum_fusion
  16.6 21.6 %collective-permute-start.3 = (f32[9,128,128]{2,1,0:T(8,128)S(1)}, f32[9,128,128]{2,1,0:T(8,128)S(1)}, u32[]{:S(2)}, u32[]{:S(2)}) collective-permute-start(f32[9,128,128]{2,1,0:T(8,128)S(1)} %get-tuple-element.15), channel_id=1, source_target_pairs={{256,0},{273,1},{290,2},{307,3},{324,4},{341,5},{358,6},{375,7},{1... | collective-permute-start | bytes 1769480 | tf_op jit(solution)/shard_map/ppermute | solution.py:18
  38.3 1.9 %collective-permute-start.5 = (f32[6,128,128]{2,1,0:T(8,128)S(1)}, f32[6,128,128]{2,1,0:T(8,128)}, u32[]{:S(2)}, u32[]{:S(2)}) collective-permute-start(f32[6,128,128]{2,1,0:T(8,128)S(1)} %bitcast_multiply_fusion.refs_3_), channel_id=1, source_target_pairs={{1,0},{2,1},{15,2},{4,3},{13,4},{6,5},{11,6},{8,7},{9,8},{10,9},{7... | collective-permute-start | bytes 1179656 | tf_op jit(solution)/shard_map/ppermute | solution.py:18
  40.2 1.9 %collective-permute-start.2 = (f32[9,128,128]{2,1,0:T(8,128)S(1)}, f32[9,128,128]{2,1,0:T(8,128)S(1)}, u32[]{:S(2)}, u32[]{:S(2)}) collective-permute-start(f32[9,128,128]{2,1,0:T(8,128)S(1)} %get-tuple-element.16), channel_id=1, source_target_pairs={{0,0},{17,1},{34,2},{51,3},{68,4},{85,5},{102,6},{119,7},{392,8},{... | collective-permute-start | bytes 1769480 | tf_op jit(solution)/shard_map/ppermute | solution.py:18
  42.1 9.6 %collective-permute-done.5 = f32[6,128,128]{2,1,0:T(8,128)} collective-permute-done((f32[6,128,128]{2,1,0:T(8,128)S(1)}, f32[6,128,128]{2,1,0:T(8,128)}, u32[]{:S(2)}, u32[]{:S(2)}) %collective-permute-start.5) | collective-permute-done | bytes 393248 | tf_op jit(solution)/shard_map/ppermute | solution.py:18
  51.7 2.3 %collective-permute-start.6 = (f32[6,128,128]{2,1,0:T(8,128)}, f32[6,128,128]{2,1,0:T(8,128)S(1)}, u32[]{:S(2)}, u32[]{:S(2)}) collective-permute-start(f32[6,128,128]{2,1,0:T(8,128)} %collective-permute-done.5), channel_id=1, source_target_pairs={{0,0},{17,1},{34,2},{51,3},{68,4},{85,5},{102,6},{119,7},{392,8},{... | collective-permute-start | bytes 1179656 | tf_op jit(solution)/shard_map/ppermute | solution.py:18
  54.1 31.7 %collective-permute-done.3 = f32[9,128,128]{2,1,0:T(8,128)S(1)} collective-permute-done((f32[9,128,128]{2,1,0:T(8,128)S(1)}, f32[9,128,128]{2,1,0:T(8,128)S(1)}, u32[]{:S(2)}, u32[]{:S(2)}) %collective-permute-start.3) | collective-permute-done | bytes 589856 | tf_op jit(solution)/shard_map/ppermute | solution.py:18
  85.7 12.8 %collective-permute-start.4 = (f32[6,128,128]{2,1,0:T(8,128)S(1)}, f32[6,128,128]{2,1,0:T(8,128)S(1)}, u32[]{:S(2)}, u32[]{:S(2)}) collective-permute-start(f32[6,128,128]{2,1,0:T(8,128)S(1)} %slice.46.refs_5_), channel_id=1, source_target_pairs={{16,0},{17,1},{18,2},{19,3},{20,4},{21,5},{22,6},{23,7},{24,8},{25... | collective-permute-start | bytes 1179656 | tf_op jit(solution)/shard_map/ppermute | solution.py:18
  98.6 6.3 %collective-permute-start.8 = (f32[6,128,128]{2,1,0:T(8,128)}, f32[6,128,128]{2,1,0:T(8,128)S(1)}, u32[]{:S(2)}, u32[]{:S(2)}) collective-permute-start(f32[6,128,128]{2,1,0:T(8,128)} %collective-permute-done.5), channel_id=1, source_target_pairs={{256,0},{273,1},{290,2},{307,3},{324,4},{341,5},{358,6},{375,7},{1... | collective-permute-start | bytes 1179656 | tf_op jit(solution)/shard_map/ppermute | solution.py:18
  104.9 16.0 %collective-permute-done.6.refs_4_ = f32[6,128,128]{2,1,0:T(8,128)S(1)} collective-permute-done((f32[6,128,128]{2,1,0:T(8,128)}, f32[6,128,128]{2,1,0:T(8,128)S(1)}, u32[]{:S(2)}, u32[]{:S(2)}) %collective-permute-start.6) | collective-permute-done | bytes 393248 | tf_op jit(solution)/shard_map/ppermute | solution.py:18
  120.9 3.1 %collective-permute-start.7 = (f32[6,128,128]{2,1,0:T(8,128)S(1)}, f32[6,128,128]{2,1,0:T(8,128)S(1)}, u32[]{:S(2)}, u32[]{:S(2)}) collective-permute-start(f32[6,128,128]{2,1,0:T(8,128)S(1)} %collective-permute-done.6.refs_4_), channel_id=1, source_target_pairs={{496,0},{497,1},{498,2},{499,3},{500,4},{501,5},{502,6},{503,7},{5... | collective-permute-start | bytes 1179656 | tf_op jit(solution)/shard_map/ppermute | solution.py:18
  124.0 0.0 collective-permute-done.2
  124.0 0.0 copy-start.1
  124.0 0.0 collective-permute-done.4.refs_5_
  124.1 0.8 copy-done.1
  124.9 0.8 pad_maximum_fusion.3
  125.6 1.9 %collective-permute-start.10 = (f32[6,128,128]{2,1,0:T(8,128)}, f32[6,128,128]{2,1,0:T(8,128)S(1)}, u32[]{:S(2)}, u32[]{:S(2)}) collective-permute-start(f32[6,128,128]{2,1,0:T(8,128)} %pad_maximum_fusion.3), channel_id=1, source_target_pairs={{1,0},{2,1},{3,2},{4,3},{5,4},{6,5},{7,6},{8,7},{9,8},{10,9},{11,1... | collective-permute-start | bytes 1179656 | tf_op jit(solution)/shard_map/ppermute | solution.py:18
  127.6 1.9 %collective-permute-start.11 = (f32[6,128,128]{2,1,0:T(8,128)S(1)}, f32[6,128,128]{2,1,0:T(8,128)S(1)}, u32[]{:S(2)}, u32[]{:S(2)}) collective-permute-start(f32[6,128,128]{2,1,0:T(8,128)S(1)} %bitcast_multiply_fusion.refs_3_), channel_id=1, source_target_pairs={{1,0},{2,1},{3,2},{4,3},{5,4},{6,5},{7,6},{8,7},{9,8},{10,9},{11,1... | collective-permute-start | bytes 1179656 | tf_op jit(solution)/shard_map/ppermute | solution.py:18
  130.0 0.1 stack.115.refs_0_
  130.1 0.1 stack.112.refs_0_
  130.1 0.1 stack.119.refs_0_
  130.2 0.1 stack.101.refs_0_
  130.3 1.0 slice.41.refs_4_
  131.3 5.8 %collective-permute-start.12 = (f32[6,128,128]{2,1,0:T(8,128)S(1)}, f32[6,128,128]{2,1,0:T(8,128)S(1)}, u32[]{:S(2)}, u32[]{:S(2)}) collective-permute-start(f32[6,128,128]{2,1,0:T(8,128)S(1)} %slice.41.refs_4_), channel_id=1, source_target_pairs={{16,0},{17,1},{18,2},{19,3},{20,4},{21,5},{22,6},{23,7},{24,8},{25... | collective-permute-start | bytes 1179656 | tf_op jit(solution)/shard_map/ppermute | solution.py:18
  137.2 0.2 broadcast_in_dim.4.refs_6_
  137.3 2.1 %shard_map.28.refs_6_ = f32[24,128,128]{2,1,0:T(8,128)S(1)} custom-call(s32[6]{0:T(128)S(1)} %stack.119.refs_0_, f32[3,128,128]{2,1,0:T(8,128)S(1)} %slice.37.refs_1_, f32[3,128,128]{2,1,0:T(8,128)S(1)} %slice.47.refs_2_, f32[6,128,128]{2,1,0:T(8,128)S(1)} %bitcast_multiply_fusion.refs_3_, f32[6,128,128]{2,1,0:T(8,128)S(1)} %slice.41.refs_4_, ...), custom_call_target="tpu_custom_call" | custom-call | flops 905969664 | bytes 4194304 | tf_op jit(solution)/shard_map/pallas_call | solution.py:109
  139.5 0.0 collective-permute-done.8.refs_5_
  139.5 0.2 collective-permute-done.7.refs_4_
  139.6 7.7 %collective-permute-start.9 = (f32[6,128,128]{2,1,0:T(8,128)S(1)}, f32[6,128,128]{2,1,0:T(8,128)S(1)}, u32[]{:S(2)}, u32[]{:S(2)}) collective-permute-start(f32[6,128,128]{2,1,0:T(8,128)S(1)} %collective-permute-done.8.refs_5_), channel_id=1, source_target_pairs={{496,0},{497,1},{498,2},{499,3},{500,4},{501,5},{502,6},{503,7},{5... | collective-permute-start | bytes 1179656 | tf_op jit(solution)/shard_map/ppermute | solution.py:18
  147.4 0.0 collective-permute-done.10
  147.4 0.0 collective-permute-done.11.refs_3_
  147.4 2.2 %shard_map.29.refs_6_ = f32[24,128,128]{2,1,0:T(8,128)S(1)} custom-call(s32[6]{0:T(128)S(1)} %stack.115.refs_0_, f32[3,128,128]{2,1,0:T(8,128)S(1)} %get-tuple-element.14.refs_1_, f32[3,128,128]{2,1,0:T(8,128)S(1)} %get-tuple-element.13.refs_2_, f32[6,128,128]{2,1,0:T(8,128)S(1)} %collective-permute-done.11.refs_3_, ...), custom_call_target="tpu_custom_call" | custom-call | flops 905969664 | bytes 4194304 | tf_op jit(solution)/shard_map/pallas_call | solution.py:109
  149.6 11.4 %collective-permute-done.12.refs_4_ = f32[6,128,128]{2,1,0:T(8,128)S(1)} collective-permute-done((f32[6,128,128]{2,1,0:T(8,128)S(1)}, f32[6,128,128]{2,1,0:T(8,128)S(1)}, u32[]{:S(2)}, u32[]{:S(2)}) %collective-permute-start.12) | collective-permute-done | bytes 393248 | tf_op jit(solution)/shard_map/ppermute | solution.py:18
  161.0 2.1 %shard_map.30.refs_6_ = f32[24,128,128]{2,1,0:T(8,128)S(1)} custom-call(s32[6]{0:T(128)S(1)} %stack.112.refs_0_, f32[3,128,128]{2,1,0:T(8,128)S(1)} %get-tuple-element.14.refs_1_, f32[3,128,128]{2,1,0:T(8,128)S(1)} %get-tuple-element.13.refs_2_, f32[6,128,128]{2,1,0:T(8,128)S(1)} %collective-permute-done.11.refs_3_, ...), custom_call_target="tpu_custom_call" | custom-call | flops 905969664 | bytes 4194304 | tf_op jit(solution)/shard_map/pallas_call | solution.py:109
  163.1 0.0 collective-permute-done.9.refs_5_
  163.1 3.3 %shard_map.31 = f32[24,128,128]{2,1,0:T(8,128)} custom-call(s32[6]{0:T(128)S(1)} %stack.101.refs_0_, f32[3,128,128]{2,1,0:T(8,128)S(1)} %slice.37.refs_1_, f32[3,128,128]{2,1,0:T(8,128)S(1)} %slice.47.refs_2_, f32[6,128,128]{2,1,0:T(8,128)S(1)} %bitcast_multiply_fusion.refs_3_, f32[6,128,128]{2,1,0:T(8,128)S(1)} %collective-permute-done.7.refs_4_, ...), custom_call_target="tpu_custom_call" | custom-call | flops 905969664 | bytes 4194304 | tf_op jit(solution)/shard_map/pallas_call | solution.py:109
  (9 shorter events, 0.2 us)
Async XLA Ops:
  0.0 2.8 %copy-start.2 = (s32[1,1,6,1]{2,3,1,0:T(1,128)S(1)}, s32[1,1,6,1]{2,3,1,0:T(1,128)}, u32[]{:S(2)}) copy-start(s32[1,1,6,1]{2,3,1,0:T(1,128)} %param.3) | copy-start | bytes 76
  0.0 2.8 %copy-start = (f32[1,1,6,1,128,128]{5,4,3,2,1,0:T(8,128)S(1)}, f32[1,1,6,1,128,128]{5,4,3,2,1,0:T(8,128)}, u32[]{:S(2)}) copy-start(f32[1,1,6,1,128,128]{5,4,3,2,1,0:T(8,128)} %param.2) | copy-start | bytes 1179652
  2.1 5.0 %collective-permute-start.1 = (f32[6,128,128]{2,1,0:T(8,128)S(1)}, f32[6,128,128]{2,1,0:T(8,128)S(1)}, u32[]{:S(2)}, u32[]{:S(2)}) collective-permute-start(f32[6,128,128]{2,1,0:T(8,128)S(1)} %pad_maximum_fusion.2), channel_id=1, source_target_pairs={{0,0},{1,1},{14,2},{3,3},{12,4},{5,5},{10,6},{7,7},{8,8},{9,9},{6,... | collective-permute-start | bytes 1179656 | tf_op jit(solution)/shard_map/ppermute | solution.py:18
  2.9 13.6 %collective-permute-start = (f32[6,128,128]{2,1,0:T(8,128)S(1)}, f32[6,128,128]{2,1,0:T(8,128)S(1)}, u32[]{:S(2)}, u32[]{:S(2)}) collective-permute-start(f32[6,128,128]{2,1,0:T(8,128)S(1)} %bitcast_multiply_fusion.refs_3_), channel_id=1, source_target_pairs={{0,0},{15,1},{2,2},{13,3},{4,4},{11,5},{6,6},{9,7},{8,8},{7,9},{10... | collective-permute-start | bytes 1179656 | tf_op jit(solution)/shard_map/ppermute | solution.py:18
  16.6 69.1 %collective-permute-start.3 = (f32[9,128,128]{2,1,0:T(8,128)S(1)}, f32[9,128,128]{2,1,0:T(8,128)S(1)}, u32[]{:S(2)}, u32[]{:S(2)}) collective-permute-start(f32[9,128,128]{2,1,0:T(8,128)S(1)} %get-tuple-element.15), channel_id=1, source_target_pairs={{256,0},{273,1},{290,2},{307,3},{324,4},{341,5},{358,6},{375,7},{1... | collective-permute-start | bytes 1769480 | tf_op jit(solution)/shard_map/ppermute | solution.py:18
  38.3 13.5 %collective-permute-start.5 = (f32[6,128,128]{2,1,0:T(8,128)S(1)}, f32[6,128,128]{2,1,0:T(8,128)}, u32[]{:S(2)}, u32[]{:S(2)}) collective-permute-start(f32[6,128,128]{2,1,0:T(8,128)S(1)} %bitcast_multiply_fusion.refs_3_), channel_id=1, source_target_pairs={{1,0},{2,1},{15,2},{4,3},{13,4},{6,5},{11,6},{8,7},{9,8},{10,9},{7... | collective-permute-start | bytes 1179656 | tf_op jit(solution)/shard_map/ppermute | solution.py:18
  40.2 83.8 %collective-permute-start.2 = (f32[9,128,128]{2,1,0:T(8,128)S(1)}, f32[9,128,128]{2,1,0:T(8,128)S(1)}, u32[]{:S(2)}, u32[]{:S(2)}) collective-permute-start(f32[9,128,128]{2,1,0:T(8,128)S(1)} %get-tuple-element.16), channel_id=1, source_target_pairs={{0,0},{17,1},{34,2},{51,3},{68,4},{85,5},{102,6},{119,7},{392,8},{... | collective-permute-start | bytes 1769480 | tf_op jit(solution)/shard_map/ppermute | solution.py:18
  51.7 69.2 %collective-permute-start.6 = (f32[6,128,128]{2,1,0:T(8,128)}, f32[6,128,128]{2,1,0:T(8,128)S(1)}, u32[]{:S(2)}, u32[]{:S(2)}) collective-permute-start(f32[6,128,128]{2,1,0:T(8,128)} %collective-permute-done.5), channel_id=1, source_target_pairs={{0,0},{17,1},{34,2},{51,3},{68,4},{85,5},{102,6},{119,7},{392,8},{... | collective-permute-start | bytes 1179656 | tf_op jit(solution)/shard_map/ppermute | solution.py:18
  85.7 38.3 %collective-permute-start.4 = (f32[6,128,128]{2,1,0:T(8,128)S(1)}, f32[6,128,128]{2,1,0:T(8,128)S(1)}, u32[]{:S(2)}, u32[]{:S(2)}) collective-permute-start(f32[6,128,128]{2,1,0:T(8,128)S(1)} %slice.46.refs_5_), channel_id=1, source_target_pairs={{16,0},{17,1},{18,2},{19,3},{20,4},{21,5},{22,6},{23,7},{24,8},{25... | collective-permute-start | bytes 1179656 | tf_op jit(solution)/shard_map/ppermute | solution.py:18
  98.6 40.9 %collective-permute-start.8 = (f32[6,128,128]{2,1,0:T(8,128)}, f32[6,128,128]{2,1,0:T(8,128)S(1)}, u32[]{:S(2)}, u32[]{:S(2)}) collective-permute-start(f32[6,128,128]{2,1,0:T(8,128)} %collective-permute-done.5), channel_id=1, source_target_pairs={{256,0},{273,1},{290,2},{307,3},{324,4},{341,5},{358,6},{375,7},{1... | collective-permute-start | bytes 1179656 | tf_op jit(solution)/shard_map/ppermute | solution.py:18
  120.9 18.7 %collective-permute-start.7 = (f32[6,128,128]{2,1,0:T(8,128)S(1)}, f32[6,128,128]{2,1,0:T(8,128)S(1)}, u32[]{:S(2)}, u32[]{:S(2)}) collective-permute-start(f32[6,128,128]{2,1,0:T(8,128)S(1)} %collective-permute-done.6.refs_4_), channel_id=1, source_target_pairs={{496,0},{497,1},{498,2},{499,3},{500,4},{501,5},{502,6},{503,7},{5... | collective-permute-start | bytes 1179656 | tf_op jit(solution)/shard_map/ppermute | solution.py:18
  124.0 0.8 copy-start.1
  125.6 21.7 %collective-permute-start.10 = (f32[6,128,128]{2,1,0:T(8,128)}, f32[6,128,128]{2,1,0:T(8,128)S(1)}, u32[]{:S(2)}, u32[]{:S(2)}) collective-permute-start(f32[6,128,128]{2,1,0:T(8,128)} %pad_maximum_fusion.3), channel_id=1, source_target_pairs={{1,0},{2,1},{3,2},{4,3},{5,4},{6,5},{7,6},{8,7},{9,8},{10,9},{11,1... | collective-permute-start | bytes 1179656 | tf_op jit(solution)/shard_map/ppermute | solution.py:18
  127.6 19.9 %collective-permute-start.11 = (f32[6,128,128]{2,1,0:T(8,128)S(1)}, f32[6,128,128]{2,1,0:T(8,128)S(1)}, u32[]{:S(2)}, u32[]{:S(2)}) collective-permute-start(f32[6,128,128]{2,1,0:T(8,128)S(1)} %bitcast_multiply_fusion.refs_3_), channel_id=1, source_target_pairs={{1,0},{2,1},{3,2},{4,3},{5,4},{6,5},{7,6},{8,7},{9,8},{10,9},{11,1... | collective-permute-start | bytes 1179656 | tf_op jit(solution)/shard_map/ppermute | solution.py:18
  131.3 29.7 %collective-permute-start.12 = (f32[6,128,128]{2,1,0:T(8,128)S(1)}, f32[6,128,128]{2,1,0:T(8,128)S(1)}, u32[]{:S(2)}, u32[]{:S(2)}) collective-permute-start(f32[6,128,128]{2,1,0:T(8,128)S(1)} %slice.41.refs_4_), channel_id=1, source_target_pairs={{16,0},{17,1},{18,2},{19,3},{20,4},{21,5},{22,6},{23,7},{24,8},{25... | collective-permute-start | bytes 1179656 | tf_op jit(solution)/shard_map/ppermute | solution.py:18
  139.6 23.5 %collective-permute-start.9 = (f32[6,128,128]{2,1,0:T(8,128)S(1)}, f32[6,128,128]{2,1,0:T(8,128)S(1)}, u32[]{:S(2)}, u32[]{:S(2)}) collective-permute-start(f32[6,128,128]{2,1,0:T(8,128)S(1)} %collective-permute-done.8.refs_5_), channel_id=1, source_target_pairs={{496,0},{497,1},{498,2},{499,3},{500,4},{501,5},{502,6},{503,7},{5... | collective-permute-start | bytes 1179656 | tf_op jit(solution)/shard_map/ppermute | solution.py:18
